TPU v7x, 512 devices: a whole 4x4x16 slice. The times are simulated.
512 devices in a mesh: dp: 32 (over z, y_lo), tensor: 16 (over x, y_hi, core).
Axes of the slice: x: 4, y: 4 (y_hi: 2, y_lo: 2; y = y_hi * 2 + y_lo), z: 16, core: 2. Of those that a mesh axis runs over, the one named last changes fastest.
Arguments:
- master: float32 [4096, 4096], P('dp', 'tensor'), may hold values from -36 to 36
- grad: float32 [4096, 4096], P('dp', 'tensor'), may hold values from -6 to 6
- moment: float32 [4096, 4096], P('dp', 'tensor'), may hold values from -4 to 4
- second: float32 [4096, 4096], P('dp', 'tensor'), may hold values from 0.1 to 2
Outputs:
- new_master: float32 [4096, 4096], P('dp', 'tensor')
- new_moment: float32 [4096, 4096], P('dp', 'tensor')
- new_second: float32 [4096, 4096], P('dp', 'tensor')
- block_scales: float32 [32, 32], P('dp', 'tensor')
- forward_copy: bfloat16 [4096, 4096], P('dp')
- transposed_copy: bfloat16 [16, 256, 4096], P(None, 'dp')
All inputs are finite; a program needn't handle non-finite values. Where the computation divides by a largest or mean magnitude, that divisor is 1e-20 or more.
Results may differ from a plain program's by a relative error of at most 0.001.
Values may be sent and summed in bfloat16 or wider, within the bound.
No kernel may reach another device: no remote copies, remote signals or barrier semaphores. Data moves between devices by JAX's collectives and lax.ppermute only.
A program may use at most 64 MiB of HBM per device.

v0:
```python
import jax
import jax.numpy as jnp
from jax import lax
from jax.sharding import PartitionSpec as P

BLOCK = 128


beta_one = 0.9
beta_two = 0.95
learn_rate = 0.01
decay_rate = 0.1
epsilon = 1e-08
scale_eps = 1e-05
correct_one = 1.0 - 0.9**10
correct_two = 1.0 - 0.95**10


def body(master, grad, moment, second):
    new_moment = beta_one * moment + (1.0 - beta_one) * grad
    new_second = beta_two * second + (1.0 - beta_two) * grad * grad
    update = (
        new_moment / correct_one / (jnp.sqrt(new_second / correct_two) + epsilon)
        + decay_rate * master
    )
    new_master = master - learn_rate * update
    height, width = new_master.shape
    blocked = new_master.reshape(height // BLOCK, BLOCK, width // BLOCK, BLOCK)
    block_scales = jnp.max(jnp.abs(blocked), axis=(1, 3)) + scale_eps
    scaled = (blocked / block_scales[:, None, :, None]).reshape(height, width).astype(jnp.bfloat16)
    forward_copy = lax.all_gather(scaled, "tensor", axis=1, tiled=True)
    flipped = scaled.T
    pieces = lax.all_to_all(flipped, "dp", split_axis=0, concat_axis=1, tiled=True)
    transposed_copy = lax.all_gather(pieces[None], "tensor", axis=0, tiled=True)
    return (new_master, new_moment, new_second, block_scales, forward_copy, transposed_copy)


def solution(mesh):
    return jax.shard_map(
        body,
        mesh=mesh,
        in_specs=(P("dp", "tensor"), P("dp", "tensor"), P("dp", "tensor"), P("dp", "tensor")),
        out_specs=(
            P("dp", "tensor"),
            P("dp", "tensor"),
            P("dp", "tensor"),
            P("dp", "tensor"),
            P("dp", None),
            P(None, "dp", None),
        ),
        check_vma=False,
    )
```

profile of v0, /device:TPU:1, one launch (start us, length us, event | category | flops | bytes accessed | tf_op | source)
XLA Modules:
  0.0 149.8 jit_solution(8138162672482682257)
XLA Ops:
  7.2 0.0 copy-start
  7.2 0.0 all-gather.3.cloned.1.call-start
  7.2 1.0 copy.39
  8.3 0.0 copy-done
  8.3 0.0 copy-start.1
  8.3 0.1 copy.34
  8.4 0.8 copy-done.1
  9.2 0.0 copy-start.2
  9.2 0.1 copy.33
  9.3 0.8 copy-done.2
  10.1 0.1 copy.35
  10.2 0.2 abs_reduce_fusion
  10.4 0.1 bitcast_reduce_fusion
  10.5 0.5 broadcast_add_fusion
  11.0 0.1 broadcast_bitcast_fusion
  11.1 0.7 divide_convert_fusion
  11.8 0.0 all-gather.3.cloned.1.call-update
  11.8 0.0 all-gather.5.cloned.1.call-start
  11.9 0.1 fusion.3
  12.0 29.6 %all_to_all.16 = bf16[32,8,128]{2,1,0:T(8,128)(2,1)} all-to-all(bf16[32,8,128]{2,1,0:T(8,128)(2,1)S(1)} %fusion.3), channel_id=1, replica_groups=mesh['dp'=32,'tensor'=16] {'dp'}, dimensions={0} | all-to-all | bytes 131072 | tf_op jit(solution)/shard_map/all_to_all | solution.py:33
  41.6 0.0 all-gather.5.cloned.1.call-update
  41.6 0.8 copy.40
  42.4 0.8 copy.41
  43.1 0.8 copy.42
  43.9 34.2 %all-gather.3.cloned.1.call-done = bf16[128,4096]{0,1:T(8,128)(2,1)} async-done(((bf16[128,256]{0,1:T(8,128)(2,1)}), bf16[128,4096]{0,1:T(8,128)(2,1)}) %all-gather.3.cloned.1.call-update) | async-done | bytes 1048592 | tf_op jit(solution)/shard_map/all_gather | solution.py:31
  78.1 2.3 %copy.43 = bf16[128,4096]{1,0:T(8,128)(2,1)} copy(bf16[128,4096]{0,1:T(8,128)(2,1)} %all-gather.3.cloned.1.call-done) | data formatting | bytes 2097152
  80.4 60.3 %all-gather.5.cloned.1.call-done = bf16[16,8,4096]{2,1,0:T(8,128)(2,1)} async-done(((bf16[1,8,4096]{2,1,0:T(8,128)(2,1)}), bf16[16,8,4096]{2,1,0:T(8,128)(2,1)}) %all-gather.5.cloned.1.call-update) | async-done | bytes 1048592 | tf_op jit(solution)/shard_map/all_gather | solution.py:34
  140.7 2.3 %copy.45 = bf16[16,8,4096]{2,1,0:T(8,128)(2,1)} copy(bf16[16,8,4096]{2,1,0:T(8,128)(2,1)} %all-gather.5.cloned.1.call-done) | data formatting | bytes 2097152
Async XLA Ops:
  7.2 1.1 copy-start
  7.2 70.9 %all-gather.3.cloned.1.call-start = ((), (), s32[]{:S(2)}) async-start(), calls=%async_computation.1 | async-start | bytes 1114112 | tf_op jit(solution)/shard_map/all_gather | solution.py:31
  8.3 0.9 copy-start.1
  9.2 0.9 copy-start.2
  11.8 128.8 %all-gather.5.cloned.1.call-start = ((), (), s32[]{:S(2)}) async-start(), calls=%async_computation.2 | async-start | bytes 1114112 | tf_op jit(solution)/shard_map/all_gather | solution.py:34
Sparse Core Ops, SparseCore 0:
  12.0 66.0 all-gather.2
  81.4 59.2 all-gather.4
where the time goes:
time: 150 us
  waiting for transfers between devices  94.5 us (63%)
  blocking collectives  29.6 us (20%)
  between operations  14.1 us (9%)
  local copies, waits for them, and re-layouts  9.78 us (7%)
  other arithmetic  1.69 us (1%)
    all_gather x1, waiting for transfers between devices, body(): transposed_copy = lax.all_gather(pieces[None], 'tensor', axis=0, tiled=True)  60.3 us
    all_gather x1, waiting for transfers between devices, body(): forward_copy = lax.all_gather(scaled, 'tensor', axis=1, tiled=True)  34.2 us
    all_to_all x1, blocking collectives, body(): lax.all_to_all(flipped, 'dp', split_axis=0, concat_axis=1, tiled=True)  29.6 us
    unnamed x15, local copies, waits for them, and re-layouts  9.71 us
  transfers between devices with their start and end apart: 2, of which 2 were waited for; matrix products, arithmetic and copies ran while one was open for 3% of the time, Pallas kernels for 0%

commit v1 on v0

v1 whole, which is shorter than its diff:
```python
import jax
import jax.numpy as jnp
from jax import lax
from jax.experimental import pallas as pl
from jax.experimental.pallas import tpu as pltpu
from jax.sharding import PartitionSpec as P

BLOCK = 128
beta_one = 0.9
beta_two = 0.95
learn_rate = 0.01
decay_rate = 0.1
epsilon = 1e-08
scale_eps = 1e-05
correct_one = 1.0 - 0.9**10
correct_two = 1.0 - 0.95**10


def step(master, grad, moment, second):
    new_moment = beta_one * moment + (1.0 - beta_one) * grad
    new_second = beta_two * second + (1.0 - beta_two) * grad * grad
    update = (
        new_moment / correct_one / (jnp.sqrt(new_second / correct_two) + epsilon)
        + decay_rate * master
    )
    return master - learn_rate * update, new_moment, new_second


def scaled_block(new_master):
    scale = jnp.max(jnp.abs(new_master)) + scale_eps
    return new_master / scale, scale


def flip_kernel(master_ref, grad_ref, moment_ref, second_ref, flip_ref):
    height, width = master_ref.shape
    for j in range(width // BLOCK):
        cols = slice(j * BLOCK, (j + 1) * BLOCK)
        new_master, _, _ = step(master_ref[:, cols], grad_ref[:, cols], moment_ref[:, cols], second_ref[:, cols])
        scaled, _ = scaled_block(new_master)
        flip_ref[cols, :] = scaled.T.astype(jnp.bfloat16)


def step_kernel(master_ref, grad_ref, moment_ref, second_ref, out_master, out_moment, out_second, scale_ref, copies_ref):
    height, width = master_ref.shape
    for j in range(width // BLOCK):
        cols = slice(j * BLOCK, (j + 1) * BLOCK)
        new_master, new_moment, new_second = step(
            master_ref[:, cols], grad_ref[:, cols], moment_ref[:, cols], second_ref[:, cols]
        )
        out_master[:, cols] = new_master
        out_moment[:, cols] = new_moment
        out_second[:, cols] = new_second
        scaled, scale = scaled_block(new_master)
        scale_ref[0, j] = scale
        low = scaled.astype(jnp.bfloat16)
        for k in range(copies_ref.shape[0]):
            copies_ref[k, :, cols] = low


def body(master, grad, moment, second):
    height, width = master.shape
    n_dp, n_tensor = lax.axis_size("dp"), lax.axis_size("tensor")
    half = n_tensor // 2
    f32, bf16 = jnp.float32, jnp.bfloat16
    whole = pl.BlockSpec(memory_space=pltpu.VMEM)
    flipped = pl.pallas_call(
        flip_kernel,
        out_shape=jax.ShapeDtypeStruct((width, height), bf16),
        in_specs=[whole] * 4,
        out_specs=whole,
        cost_estimate=pl.CostEstimate(flops=20 * height * width, bytes_accessed=16 * height * width, transcendentals=0),
        name="flip",
    )(master, grad, moment, second)
    same = jax.ShapeDtypeStruct((height, width), f32)
    new_master, new_moment, new_second, block_scales, copies = pl.pallas_call(
        step_kernel,
        out_shape=(same, same, same, jax.ShapeDtypeStruct((1, width // BLOCK), f32), jax.ShapeDtypeStruct((half, height, width), bf16)),
        in_specs=[whole] * 4,
        out_specs=(whole, whole, whole, pl.BlockSpec(memory_space=pltpu.SMEM), whole),
        cost_estimate=pl.CostEstimate(flops=20 * height * width, bytes_accessed=48 * height * width, transcendentals=0),
        name="step",
    )(master, grad, moment, second)
    same_core = [[2 * i + c for i in range(half)] for c in range(2)]
    swap = [(i, i ^ 1) for i in range(n_tensor)]
    pieces = lax.all_to_all(flipped.reshape(n_dp, width // n_dp, height), "dp", 0, 0, tiled=True)
    mine_f = lax.all_to_all(copies, "tensor", 0, 0, tiled=True, axis_index_groups=same_core)
    mine_t = lax.all_to_all(jnp.broadcast_to(pieces[None], (half, *pieces.shape)), "tensor", 0, 0, tiled=True, axis_index_groups=same_core)
    other_f = lax.ppermute(mine_f, "tensor", swap)
    other_t = lax.ppermute(mine_t, "tensor", swap)
    first = lax.axis_index("tensor") % 2 == 0
    both_f = jnp.where(first, jnp.stack([mine_f, other_f], 1), jnp.stack([other_f, mine_f], 1))
    forward_copy = both_f.reshape(n_tensor, height, width).transpose(1, 0, 2).reshape(height, n_tensor * width)
    both_t = jnp.where(first, jnp.stack([mine_t, other_t], 1), jnp.stack([other_t, mine_t], 1))
    transposed_copy = both_t.reshape(n_tensor, n_dp, width // n_dp, height).transpose(0, 2, 1, 3).reshape(n_tensor, width // n_dp, n_dp * height)
    return (new_master, new_moment, new_second, block_scales, forward_copy, transposed_copy)


def solution(mesh):
    spec = P("dp", "tensor")
    return jax.shard_map(
        body,
        mesh=mesh,
        in_specs=(spec,) * 4,
        out_specs=(spec, spec, spec, spec, P("dp", None), P(None, "dp", None)),
        check_vma=False,
    )
```

time: 150 us -> 70.9 us (0.47)
  waiting for transfers between devices: 94.5 us -> 13.4 us
  starting transfers between devices: 0.08 us -> 32.7 us
  blocking collectives: 29.6 us -> 15.2 us
  between operations: 14.1 us -> 0.72 us
  local copies, waits for them, and re-layouts: 9.78 us -> 2.92 us
  Pallas kernels: 0 us -> 4.26 us
    all_gather x2 -> x0, waiting for transfers between devices: 94.5 us -> none  [the longest x1 60.3 us: body(): transposed_copy = lax.all_gather(pieces[None], 'tensor', axis=0, tiled=True)]
    all_to_all x0 -> x2, starting transfers between devices: none -> 20.5 us  [the longest x1 17 us: body(): lax.all_to_all(flipped.reshape(n_dp, width // n_dp, height), 'dp', 0, 0,...]
    all_to_all x1, blocking collectives: 29.6 us -> 15.2 us  [body(): lax.all_to_all(copies, 'tensor', 0, 0, tiled=True, axis_index_groups=same...]
    all_to_all x0 -> x2, waiting for transfers between devices: none -> 13.4 us  [the longest x1 10.4 us: body(): lax.all_to_all(flipped.reshape(n_dp, width // n_dp, height), 'dp', 0, 0,...]
    ppermute x0 -> x2, starting transfers between devices: none -> 12.2 us  [the longest x1 6.64 us: body(): other_t = lax.ppermute(mine_t, 'tensor', swap)]
    unnamed x15 -> x1, local copies, waits for them, and re-layouts: 9.71 us -> 1.31 us
    pallas_call x0 -> x2, Pallas kernels: none -> 4.26 us  [the longest x1 2.19 us: body(): pl.pallas_call(step_kernel, out_shape=(same, same, same, jax.ShapeDtypeSt...]
  transfers between devices with their start and end apart: 2 -> 4, of which waited for: 2 -> 2; matrix products, arithmetic and copies ran while one was open for 3% -> 3% of each run, Pallas kernels for 0% -> 3%
where the time goes in v1:
time: 70.9 us; the launch traced here: 70.4 us
  starting transfers between devices  32.7 us (46%)
  blocking collectives  15.2 us (21%)
  waiting for transfers between devices  13.4 us (19%)
  Pallas kernels  4.26 us (6%)
  local copies, waits for them, and re-layouts  2.92 us (4%)
  other arithmetic  1.24 us (2%)
  between operations  0.72 us (1%)
    all_to_all x1, starting transfers between devices, body(): lax.all_to_all(flipped.reshape(n_dp, width // n_dp, height), 'dp', 0, 0,...  17 us
    all_to_all x1, blocking collectives, body(): lax.all_to_all(copies, 'tensor', 0, 0, tiled=True, axis_index_groups=same...  15.2 us
    all_to_all x1, waiting for transfers between devices, body(): lax.all_to_all(flipped.reshape(n_dp, width // n_dp, height), 'dp', 0, 0,...  10.4 us
    ppermute x1, starting transfers between devices, body(): other_t = lax.ppermute(mine_t, 'tensor', swap)  6.64 us
    ppermute x1, starting transfers between devices, body(): other_f = lax.ppermute(mine_f, 'tensor', swap)  5.54 us
    all_to_all x1, starting transfers between devices, body(): lax.all_to_all(jnp.broadcast_to(pieces[None], (half, *pieces.shape)), 'te...  3.49 us
    all_to_all x1, waiting for transfers between devices, body(): lax.all_to_all(jnp.broadcast_to(pieces[None], (half, *pieces.shape)), 'te...  2.93 us
    pallas_call x1, Pallas kernels, body(): pl.pallas_call(step_kernel, out_shape=(same, same, same, jax.ShapeDtypeSt...  2.19 us
  transfers between devices with their start and end apart: 4, of which 2 were waited for; matrix products, arithmetic and copies ran while one was open for 3% of the time, Pallas kernels for 3%

profile of v1, /device:TPU:1, one launch (start us, length us, event | category | flops | bytes accessed | tf_op | source)
XLA Modules:
  0.0 70.4 jit_solution(17655170622259500482)
XLA Ops:
  0.6 2.1 %flip.1 = bf16[256,128]{1,0:T(8,128)(2,1)} custom-call(f32[128,256]{1,0:T(8,128)} %master_ref.3, f32[128,256]{1,0:T(8,128)} %grad_ref.3, f32[128,256]{1,0:T(8,128)} %moment_ref.3, f32[128,256]{1,0:T(8,128)} %second_ref.3), custom_call_target="tpu_custom_call" | custom-call | flops 655360 | bytes 524288 | tf_op jit(solution)/shard_map/flip/pallas_call | solution.py:66
  2.7 17.0 %all-to-all-start.1 = ((bf16[32,8,128]{2,1,0:T(8,128)(2,1)}), bf16[32,8,128]{2,1,0:T(8,128)(2,1)S(1)}, u32[]{:S(2)}, u32[]{:S(2)}) async-start(bf16[32,8,128]{2,1,0:T(8,128)(2,1)} %bitcast.21), calls=%async_computation.1 | async-start | bytes 131072 | tf_op jit(solution)/shard_map/all_to_all | solution.py:85
  19.8 2.2 %step.1 = (f32[128,256]{1,0:T(8,128)}, f32[128,256]{1,0:T(8,128)}, f32[128,256]{1,0:T(8,128)}, f32[1,2]{1,0:T(1,128)}, bf16[8,128,256]{2,1,0:T(8,128)(2,1)}) custom-call(f32[128,256]{1,0:T(8,128)} %master_ref.3, f32[128,256]{1,0:T(8,128)} %grad_ref.3, f32[128,256]{1,0:T(8,128)} %moment_ref.3, f32[128,256]{1,0:T(8,128)} %second_ref.3), custom_call_target="tpu_custom_call" | custom-call | flops 655360 | bytes 1572864 | tf_op jit(solution)/shard_map/step/pallas_call | solution.py:75
  21.9 10.4 %all-to-all-done.1 = bf16[32,8,128]{2,1,0:T(8,128)(2,1)S(1)} async-done(((bf16[32,8,128]{2,1,0:T(8,128)(2,1)}), bf16[32,8,128]{2,1,0:T(8,128)(2,1)S(1)}, u32[]{:S(2)}, u32[]{:S(2)}) %all-to-all-start.1) | async-done | bytes 65568 | tf_op jit(solution)/shard_map/all_to_all | solution.py:85
  32.4 15.2 %all_to_all.15 = bf16[8,128,256]{2,1,0:T(8,128)(2,1)S(1)} all-to-all(bf16[8,128,256]{2,1,0:T(8,128)(2,1)} %get-tuple-element.15), channel_id=1, replica_groups={{0,2,4,6,8,10,12,14},{1,3,5,7,9,11,13,15},{16,18,20,22,24,26,28,30},{17..., dimensions={0} | all-to-all | bytes 1048576 | tf_op jit(solution)/shard_map/all_to_all | solution.py:86
  47.6 0.9 %broadcast_in_dim.2 = bf16[8,32,8,128]{3,2,1,0:T(8,128)(2,1)} broadcast(bf16[32,8,128]{2,1,0:T(8,128)(2,1)S(1)} %all-to-all-done.1), dimensions={1,2,3} | broadcast | bytes 589824 | tf_op jit(solution)/shard_map/broadcast_in_dim | solution.py:87
  48.5 3.5 %all-to-all-start.2 = ((bf16[8,32,8,128]{3,2,1,0:T(8,128)(2,1)}), bf16[8,32,8,128]{3,2,1,0:T(8,128)(2,1)S(1)}, u32[]{:S(2)}, u32[]{:S(2)}) async-start(bf16[8,32,8,128]{3,2,1,0:T(8,128)(2,1)} %broadcast_in_dim.2), calls=%async_computation.2 | async-start | bytes 1048576 | tf_op jit(solution)/shard_map/all_to_all | solution.py:87
  52.0 5.5 %collective-permute-start = (bf16[8,128,256]{2,1,0:T(8,128)(2,1)S(1)}, bf16[8,128,256]{2,1,0:T(8,128)(2,1)S(1)}, u32[]{:S(2)}, u32[]{:S(2)}) collective-permute-start(bf16[8,128,256]{2,1,0:T(8,128)(2,1)S(1)} %all_to_all.15), channel_id=1, source_target_pairs={{0,1},{1,0},{2,3},{3,2},{4,5},{5,4},{6,7},{7,6},{8,9},{9,8},{10,11... | collective-permute-start | bytes 1572872 | tf_op jit(solution)/shard_map/ppermute | solution.py:88
  57.5 2.9 %all-to-all-done.2 = bf16[8,32,8,128]{3,2,1,0:T(8,128)(2,1)S(1)} async-done(((bf16[8,32,8,128]{3,2,1,0:T(8,128)(2,1)}), bf16[8,32,8,128]{3,2,1,0:T(8,128)(2,1)S(1)}, u32[]{:S(2)}, u32[]{:S(2)}) %all-to-all-start.2) | async-done | bytes 524320 | tf_op jit(solution)/shard_map/all_to_all | solution.py:87
  60.4 6.6 %collective-permute-start.1 = (bf16[8,32,8,128]{3,2,1,0:T(8,128)(2,1)S(1)}, bf16[8,32,8,128]{3,2,1,0:T(8,128)(2,1)S(1)}, u32[]{:S(2)}, u32[]{:S(2)}) collective-permute-start(bf16[8,32,8,128]{3,2,1,0:T(8,128)(2,1)S(1)} %all-to-all-done.2), channel_id=1, source_target_pairs={{0,1},{1,0},{2,3},{3,2},{4,5},{5,4},{6,7},{7,6},{8,9},{9,8},{10,11... | collective-permute-start | bytes 1572872 | tf_op jit(solution)/shard_map/ppermute | solution.py:89
  67.1 0.0 collective-permute-done
  67.1 0.2 maximum_select_fusion
  67.3 0.1 copy.11
  67.4 0.7 copy.12
  68.1 1.3 %copy.13 = bf16[128,4096]{1,0:T(8,128)(2,1)} copy(bf16[128,4096]{0,1:T(8,128)(2,1)S(1)} %bitcast.15) | data formatting | bytes 2097152
  69.4 0.0 collective-permute-done.1
  69.4 1.1 %maximum_select_fusion.1 = bf16[8,2,32,8,128]{4,3,2,1,0:T(8,128)(2,1)} fusion(bf16[8,1,32,8,128]{4,3,2,1,0:T(8,128)(2,1)S(1)} %bitcast.19, bf16[8,1,32,8,128]{4,3,2,1,0:T(8,128)(2,1)S(1)} %bitcast.16, pred[]{:T(512)S(6)} %eq.5), kind=kLoop, calls=%fused_computation.1 | loop fusion | flops 1572864 | bytes 2097153 | tf_op jit(solution)/shard_map/jit(_where)/select_n | solution.py:93
Async XLA Ops:
  2.7 29.7 %all-to-all-start.1 = ((bf16[32,8,128]{2,1,0:T(8,128)(2,1)}), bf16[32,8,128]{2,1,0:T(8,128)(2,1)S(1)}, u32[]{:S(2)}, u32[]{:S(2)}) async-start(bf16[32,8,128]{2,1,0:T(8,128)(2,1)} %bitcast.21), calls=%async_computation.1 | async-start | bytes 131072 | tf_op jit(solution)/shard_map/all_to_all | solution.py:85
  48.5 12.0 %all-to-all-start.2 = ((bf16[8,32,8,128]{3,2,1,0:T(8,128)(2,1)}), bf16[8,32,8,128]{3,2,1,0:T(8,128)(2,1)S(1)}, u32[]{:S(2)}, u32[]{:S(2)}) async-start(bf16[8,32,8,128]{3,2,1,0:T(8,128)(2,1)} %broadcast_in_dim.2), calls=%async_computation.2 | async-start | bytes 1048576 | tf_op jit(solution)/shard_map/all_to_all | solution.py:87
  52.0 15.1 %collective-permute-start = (bf16[8,128,256]{2,1,0:T(8,128)(2,1)S(1)}, bf16[8,128,256]{2,1,0:T(8,128)(2,1)S(1)}, u32[]{:S(2)}, u32[]{:S(2)}) collective-permute-start(bf16[8,128,256]{2,1,0:T(8,128)(2,1)S(1)} %all_to_all.15), channel_id=1, source_target_pairs={{0,1},{1,0},{2,3},{3,2},{4,5},{5,4},{6,7},{7,6},{8,9},{9,8},{10,11... | collective-permute-start | bytes 1572872 | tf_op jit(solution)/shard_map/ppermute | solution.py:88
  60.4 8.9 %collective-permute-start.1 = (bf16[8,32,8,128]{3,2,1,0:T(8,128)(2,1)S(1)}, bf16[8,32,8,128]{3,2,1,0:T(8,128)(2,1)S(1)}, u32[]{:S(2)}, u32[]{:S(2)}) collective-permute-start(bf16[8,32,8,128]{3,2,1,0:T(8,128)(2,1)S(1)} %all-to-all-done.2), channel_id=1, source_target_pairs={{0,1},{1,0},{2,3},{3,2},{4,5},{5,4},{6,7},{7,6},{8,9},{9,8},{10,11... | collective-permute-start | bytes 1572872 | tf_op jit(solution)/shard_map/ppermute | solution.py:89

commit v2 on v1

v2 whole, which is shorter than its diff:
```python
import jax
import jax.numpy as jnp
from jax import lax
from jax.experimental import pallas as pl
from jax.experimental.pallas import tpu as pltpu
from jax.sharding import PartitionSpec as P

BLOCK = 128
beta_one = 0.9
beta_two = 0.95
learn_rate = 0.01
decay_rate = 0.1
epsilon = 1e-08
scale_eps = 1e-05
correct_one = 1.0 - 0.9**10
correct_two = 1.0 - 0.95**10


def step(master, grad, moment, second):
    new_moment = beta_one * moment + (1.0 - beta_one) * grad
    new_second = beta_two * second + (1.0 - beta_two) * grad * grad
    update = (
        new_moment / correct_one / (jnp.sqrt(new_second / correct_two) + epsilon)
        + decay_rate * master
    )
    return master - learn_rate * update, new_moment, new_second


def scaled_block(new_master):
    scale = jnp.max(jnp.abs(new_master)) + scale_eps
    return new_master / scale, scale


def visit(n, first):
    rest = [k for k in range(n) if k != first]
    return [first] + sorted(rest, key=lambda k: (-min(abs(k - first), n - abs(k - first)), k))


def flip_kernel(order, master_ref, grad_ref, moment_ref, second_ref, flip_ref, low_ref):
    height, width = master_ref.shape
    rows = width // len(order)
    for j in range(width // BLOCK):
        cols = slice(j * BLOCK, (j + 1) * BLOCK)
        new_master, _, _ = step(master_ref[:, cols], grad_ref[:, cols], moment_ref[:, cols], second_ref[:, cols])
        scaled, _ = scaled_block(new_master)
        flipped = scaled.T.astype(jnp.bfloat16)
        for k, owner in enumerate(order):
            if owner * rows // BLOCK == j:
                at = owner * rows - j * BLOCK
                flip_ref[k * rows : (k + 1) * rows, :] = flipped[at : at + rows]
        low_ref[j * height : (j + 1) * height, :] = scaled.astype(jnp.bfloat16)


def step_kernel(master_ref, grad_ref, moment_ref, second_ref, low_ref, out_master, out_moment, out_second, scale_ref, both_ref, sem):
    rows = low_ref.shape[0]
    copies = [pltpu.make_async_copy(low_ref, both_ref.at[k, :rows], sem) for k in range(both_ref.shape[0])]
    for copy in copies:
        copy.start()
    height, width = master_ref.shape
    for j in range(width // BLOCK):
        cols = slice(j * BLOCK, (j + 1) * BLOCK)
        new_master, new_moment, new_second = step(
            master_ref[:, cols], grad_ref[:, cols], moment_ref[:, cols], second_ref[:, cols]
        )
        out_master[:, cols] = new_master
        out_moment[:, cols] = new_moment
        out_second[:, cols] = new_second
        _, scale = scaled_block(new_master)
        scale_ref[0, j] = scale
    for copy in copies:
        copy.wait()


def pack_kernel(order, pieces_ref, _, both_ref, slab, sem):
    rows = pieces_ref.shape[0]
    part = rows // len(order)
    for k, owner in enumerate(order):
        slab[owner * part : (owner + 1) * part, :] = pieces_ref[k * part : (k + 1) * part, :]
    copies = [pltpu.make_async_copy(slab, both_ref.at[k, rows:], sem) for k in range(both_ref.shape[0])]
    for copy in copies:
        copy.start()
    for copy in copies:
        copy.wait()


def place_kernel(order, flip, both_ref, *refs):
    forward_ref, flipped_ref, sem = refs[-3:]
    chips, rows2, _ = both_ref.shape
    rows = rows2 // 2
    height = forward_ref.shape[0]
    width = rows * BLOCK // height
    core = (lax.axis_index("tensor") & 1) ^ flip
    copies = []
    for k, chip in enumerate(order):
        slab = 2 * chip + core
        copies.append(pltpu.make_async_copy(both_ref.at[k, rows:, :], flipped_ref.at[slab], sem))
        for j in range(width // BLOCK):
            start = pl.multiple_of(slab * width + j * BLOCK, BLOCK)
            copies.append(
                pltpu.make_async_copy(
                    both_ref.at[k, j * height : (j + 1) * height, :], forward_ref.at[:, pl.ds(start, BLOCK)], sem
                )
            )
    for copy in copies:
        copy.start()
    for copy in copies:
        copy.wait()


def in_vmem(x):
    return pltpu.with_memory_space_constraint(x, pltpu.VMEM)


whole = pl.BlockSpec(memory_space=pltpu.VMEM)
hbm = pl.BlockSpec(memory_space=pl.ANY)


def place(order, flip, both, height, n_tensor, outs):
    rows = both.shape[1] // 2
    width = rows * BLOCK // height
    return pl.pallas_call(
        lambda *refs: place_kernel(order, flip, *refs),
        out_shape=(
            jax.ShapeDtypeStruct((height, n_tensor * width), jnp.bfloat16),
            jax.ShapeDtypeStruct((n_tensor, rows, BLOCK), jnp.bfloat16),
        ),
        in_specs=[whole] + [hbm] * len(outs),
        out_specs=(hbm, hbm),
        scratch_shapes=[pltpu.SemaphoreType.DMA],
        input_output_aliases={1 + i: i for i in range(len(outs))},
        cost_estimate=pl.CostEstimate(flops=0, bytes_accessed=4 * both.size, transcendentals=0),
        name="place_other" if flip else "place_mine",
    )(in_vmem(both), *outs)


def body(master, grad, moment, second):
    height, width = master.shape
    n_dp, n_tensor = lax.axis_size("dp"), lax.axis_size("tensor")
    half = n_tensor // 2
    f32, bf16 = jnp.float32, jnp.bfloat16
    rows = height * width // BLOCK
    z_order = visit(n_dp // 2, n_dp // 4)
    chip_order = visit(half, half // 2 + 1)
    flipped, low = pl.pallas_call(
        lambda *refs: flip_kernel(z_order, *refs),
        out_shape=(jax.ShapeDtypeStruct((width, height), bf16), jax.ShapeDtypeStruct((rows, BLOCK), bf16)),
        in_specs=[whole] * 4,
        out_specs=(whole, whole),
        cost_estimate=pl.CostEstimate(flops=20 * height * width, bytes_accessed=16 * height * width, transcendentals=0),
        name="flip",
    )(master, grad, moment, second)
    same = jax.ShapeDtypeStruct((height, width), f32)
    new_master, new_moment, new_second, block_scales, both = pl.pallas_call(
        step_kernel,
        out_shape=(same, same, same, jax.ShapeDtypeStruct((1, width // BLOCK), f32), jax.ShapeDtypeStruct((half, 2 * rows, BLOCK), bf16)),
        in_specs=[whole] * 5,
        out_specs=(whole, whole, whole, pl.BlockSpec(memory_space=pltpu.SMEM), hbm),
        scratch_shapes=[pltpu.SemaphoreType.DMA],
        cost_estimate=pl.CostEstimate(flops=20 * height * width, bytes_accessed=30 * height * width, transcendentals=0),
        name="step",
    )(master, grad, moment, second, low)
    dp_order = [[2 * z + y for z in z_order for y in range(2)]]
    pieces = lax.all_to_all(flipped.reshape(n_dp, width // n_dp, height), "dp", 0, 0, tiled=True, axis_index_groups=dp_order)
    both = pl.pallas_call(
        lambda *refs: pack_kernel(z_order, *refs),
        out_shape=jax.ShapeDtypeStruct(both.shape, bf16),
        in_specs=[whole, hbm],
        out_specs=hbm,
        scratch_shapes=[pltpu.VMEM((rows, BLOCK), bf16), pltpu.SemaphoreType.DMA],
        input_output_aliases={1: 0},
        name="pack",
    )(in_vmem(pieces.reshape(rows, BLOCK)), both)
    same_core = [[2 * k + c for k in chip_order] for c in range(2)]
    mine = lax.all_to_all(both, "tensor", 0, 0, tiled=True, axis_index_groups=same_core)
    other = lax.ppermute(mine, "tensor", [(i, i ^ 1) for i in range(n_tensor)])
    outs = place(chip_order, 0, mine, height, n_tensor, ())
    forward_copy, slabs = place(chip_order, 1, other, height, n_tensor, outs)
    transposed_copy = slabs.reshape(n_tensor, n_dp, width // n_dp, height).transpose(0, 2, 1, 3).reshape(n_tensor, width // n_dp, n_dp * height)
    return (new_master, new_moment, new_second, block_scales, forward_copy, transposed_copy)


def solution(mesh):
    spec = P("dp", "tensor")
    return jax.shard_map(
        body,
        mesh=mesh,
        in_specs=(spec,) * 4,
        out_specs=(spec, spec, spec, spec, P("dp", None), P(None, "dp", None)),
        check_vma=False,
    )
```

time: 70.9 us -> 55 us (0.78)
  waiting for transfers between devices: 13.4 us -> 2.59 us
  starting transfers between devices: 32.7 us -> 24.4 us
  blocking collectives: 15.2 us -> 19.7 us
  Pallas kernels: 4.26 us -> 7.4 us
  local copies, waits for them, and re-layouts: 2.92 us -> 0 us
  other arithmetic: 1.24 us -> 0 us
    all_to_all x1, waiting for transfers between devices: 10.4 us -> 1.29 us  [body(): lax.all_to_all(flipped.reshape(n_dp, width // n_dp, height), 'dp', 0, 0,...]
    ppermute x2 -> x1, starting transfers between devices: 12.2 us -> 4.09 us  [body(): other = lax.ppermute(mine, 'tensor', [(i, i ^ 1) for i in range(n_tensor)])]
    all_to_all x1, blocking collectives: 15.2 us -> 19.7 us  [body(): lax.all_to_all(both, 'tensor', 0, 0, tiled=True, axis_index_groups=same_c...]
    all_to_all x1 -> x0, starting transfers between devices: 3.49 us -> none  [body(): lax.all_to_all(jnp.broadcast_to(pieces[None], (half, *pieces.shape)), 'te...]
    all_to_all x1, starting transfers between devices: 17 us -> 20.3 us  [body(): lax.all_to_all(flipped.reshape(n_dp, width // n_dp, height), 'dp', 0, 0,...]
    all_to_all x1 -> x0, waiting for transfers between devices: 2.93 us -> none  [body(): lax.all_to_all(jnp.broadcast_to(pieces[None], (half, *pieces.shape)), 'te...]
    pallas_call x1 -> x4, Pallas kernels: 2.07 us -> 4.77 us  [the longest x1 2.07 us: body(): pl.pallas_call(lambda *refs: flip_kernel(z_order, *refs), out_shape=(jax....]
    unnamed x1 -> x0, local copies, waits for them, and re-layouts: 1.31 us -> none
  transfers between devices with their start and end apart: 4 -> 2, of which waited for: 2 -> 2; matrix products, arithmetic and copies ran while one was open for 3% -> 0% of each run, Pallas kernels for 3% -> 7%
where the time goes in v2:
time: 55 us; the launch traced here: 54.8 us
  starting transfers between devices  24.4 us (44%)
  blocking collectives  19.7 us (36%)
  Pallas kernels  7.4 us (13%)
  waiting for transfers between devices  2.59 us (5%)
  between operations  0.67 us (1%)
    all_to_all x1, starting transfers between devices, body(): lax.all_to_all(flipped.reshape(n_dp, width // n_dp, height), 'dp', 0, 0,...  20.3 us
    all_to_all x1, blocking collectives, body(): lax.all_to_all(both, 'tensor', 0, 0, tiled=True, axis_index_groups=same_c...  19.7 us
    ppermute x1, starting transfers between devices, body(): other = lax.ppermute(mine, 'tensor', [(i, i ^ 1) for i in range(n_tensor)])  4.09 us
    pallas_call x1, Pallas kernels, body(): pl.pallas_call(step_kernel, out_shape=(same, same, same, jax.ShapeDtypeSt...  2.63 us
    pallas_call x1, Pallas kernels, body(): pl.pallas_call(lambda *refs: flip_kernel(z_order, *refs), out_shape=(jax....  2.07 us
    pallas_call x2, Pallas kernels, place(): pl.pallas_call(lambda *refs: place_kernel(order, flip, *refs), out_shape=...  1.91 us
    ppermute x1, waiting for transfers between devices, body(): other = lax.ppermute(mine, 'tensor', [(i, i ^ 1) for i in range(n_tensor)])  1.3 us
    all_to_all x1, waiting for transfers between devices, body(): lax.all_to_all(flipped.reshape(n_dp, width // n_dp, height), 'dp', 0, 0,...  1.29 us
  transfers between devices with their start and end apart: 2, of which 2 were waited for; matrix products, arithmetic and copies ran while one was open for 0% of the time, Pallas kernels for 7%

profile of v2, /device:TPU:1, one launch (start us, length us, event | category | flops | bytes accessed | tf_op | source)
XLA Modules:
  0.0 54.8 jit_solution(14701991355923778517)
XLA Ops:
  0.6 2.1 %flip.1 = (bf16[256,128]{1,0:T(8,128)(2,1)}, bf16[256,128]{1,0:T(8,128)(2,1)}) custom-call(f32[128,256]{1,0:T(8,128)} %master_ref.1, f32[128,256]{1,0:T(8,128)} %grad_ref.1, f32[128,256]{1,0:T(8,128)} %moment_ref.1, f32[128,256]{1,0:T(8,128)} %second_ref.1), custom_call_target="tpu_custom_call" | custom-call | flops 655360 | bytes 524288 | tf_op jit(solution)/shard_map/flip/pallas_call | solution.py:144
  2.7 20.3 %all-to-all-start = ((bf16[32,8,128]{2,1,0:T(8,128)(2,1)}), bf16[32,8,128]{2,1,0:T(8,128)(2,1)S(1)}, u32[]{:S(2)}, u32[]{:S(2)}) async-start(bf16[32,8,128]{2,1,0:T(8,128)(2,1)} %bitcast.9), calls=%async_computation | async-start | bytes 131072 | tf_op jit(solution)/shard_map/all_to_all | solution.py:163
  23.0 2.6 %step.1 = (f32[128,256]{1,0:T(8,128)}, f32[128,256]{1,0:T(8,128)}, f32[128,256]{1,0:T(8,128)}, f32[1,2]{1,0:T(1,128)}, bf16[8,512,128]{2,1,0:T(8,128)(2,1)}) custom-call(f32[128,256]{1,0:T(8,128)} %master_ref.1, f32[128,256]{1,0:T(8,128)} %grad_ref.1, f32[128,256]{1,0:T(8,128)} %moment_ref.1, f32[128,256]{1,0:T(8,128)} %second_ref.1, ...), custom_call_target="tpu_custom_call" | custom-call | flops 655360 | bytes 983040 | tf_op jit(solution)/shard_map/step/pallas_call | solution.py:153
  25.6 1.3 %all-to-all-done = bf16[32,8,128]{2,1,0:T(8,128)(2,1)S(1)} async-done(((bf16[32,8,128]{2,1,0:T(8,128)(2,1)}), bf16[32,8,128]{2,1,0:T(8,128)(2,1)S(1)}, u32[]{:S(2)}, u32[]{:S(2)}) %all-to-all-start) | async-done | bytes 65568 | tf_op jit(solution)/shard_map/all_to_all | solution.py:163
  26.9 0.8 %pack.1 = bf16[8,512,128]{2,1,0:T(8,128)(2,1)} custom-call(bf16[256,128]{1,0:T(8,128)(2,1)S(1)} %bitcast.7, bf16[8,512,128]{2,1,0:T(8,128)(2,1)} %get-tuple-element.23.refs_1_), custom_call_target="tpu_custom_call", output_to_operand_aliasing={{}: (1, {})} | custom-call | tf_op jit(solution)/shard_map/pack/pallas_call | solution.py:164
  27.7 19.7 %all_to_all.10.refs_0_ = bf16[8,512,128]{2,1,0:T(8,128)(2,1)S(1)} all-to-all(bf16[8,512,128]{2,1,0:T(8,128)(2,1)} %pack.1), channel_id=1, replica_groups={{10,2,0,4,6,14,8,12},{11,3,1,5,7,15,9,13},{26,18,16,20,22,30,24,28},{27..., dimensions={0} | all-to-all | bytes 2097152 | tf_op jit(solution)/shard_map/all_to_all | solution.py:174
  47.4 4.1 %collective-permute-start = (bf16[8,512,128]{2,1,0:T(8,128)(2,1)S(1)}, bf16[8,512,128]{2,1,0:T(8,128)(2,1)S(1)}, u32[]{:S(2)}, u32[]{:S(2)}) collective-permute-start(bf16[8,512,128]{2,1,0:T(8,128)(2,1)S(1)} %all_to_all.10.refs_0_), channel_id=1, source_target_pairs={{0,1},{1,0},{2,3},{3,2},{4,5},{5,4},{6,7},{7,6},{8,9},{9,8},{10,11... | collective-permute-start | bytes 3145736 | tf_op jit(solution)/shard_map/ppermute | solution.py:175
  51.5 1.0 %place_mine.1 = (bf16[128,4096]{1,0:T(8,128)(2,1)}, bf16[16,256,128]{2,1,0:T(8,128)(2,1)}) custom-call(bf16[8,512,128]{2,1,0:T(8,128)(2,1)S(1)} %all_to_all.10.refs_0_), custom_call_target="tpu_custom_call" | custom-call | bytes 2097152 | tf_op jit(solution)/shard_map/place_mine/pallas_call | solution.py:121
  52.5 1.3 %collective-permute-done.refs_0_ = bf16[8,512,128]{2,1,0:T(8,128)(2,1)S(1)} collective-permute-done((bf16[8,512,128]{2,1,0:T(8,128)(2,1)S(1)}, bf16[8,512,128]{2,1,0:T(8,128)(2,1)S(1)}, u32[]{:S(2)}, u32[]{:S(2)}) %collective-permute-start) | collective-permute-done | bytes 1048608 | tf_op jit(solution)/shard_map/ppermute | solution.py:175
  53.8 0.9 %place_other.1 = (bf16[128,4096]{1,0:T(8,128)(2,1)}, bf16[16,256,128]{2,1,0:T(8,128)(2,1)}) custom-call(bf16[8,512,128]{2,1,0:T(8,128)(2,1)S(1)} %collective-permute-done.refs_0_, bf16[128,4096]{1,0:T(8,128)(2,1)} %get-tuple-element.24.refs_1_, bf16[16,256,128]{2,1,0:T(8,128)(2,1)} %get-tuple-element.25.refs_2_), custom_call_target="tpu_custom_call", output_to_operand_aliasing={{0}: (1, {}), {1}: (2, {})} | custom-call | bytes 2097152 | tf_op jit(solution)/shard_map/place_other/pallas_call | solution.py:121
Async XLA Ops:
  2.7 24.2 %all-to-all-start = ((bf16[32,8,128]{2,1,0:T(8,128)(2,1)}), bf16[32,8,128]{2,1,0:T(8,128)(2,1)S(1)}, u32[]{:S(2)}, u32[]{:S(2)}) async-start(bf16[32,8,128]{2,1,0:T(8,128)(2,1)} %bitcast.9), calls=%async_computation | async-start | bytes 131072 | tf_op jit(solution)/shard_map/all_to_all | solution.py:163
  47.4 6.4 %collective-permute-start = (bf16[8,512,128]{2,1,0:T(8,128)(2,1)S(1)}, bf16[8,512,128]{2,1,0:T(8,128)(2,1)S(1)}, u32[]{:S(2)}, u32[]{:S(2)}) collective-permute-start(bf16[8,512,128]{2,1,0:T(8,128)(2,1)S(1)} %all_to_all.10.refs_0_), channel_id=1, source_target_pairs={{0,1},{1,0},{2,3},{3,2},{4,5},{5,4},{6,7},{7,6},{8,9},{9,8},{10,11... | collective-permute-start | bytes 3145736 | tf_op jit(solution)/shard_map/ppermute | solution.py:175

commit v3 on v1

v3 whole, which is shorter than its diff:
```python
import jax
import jax.numpy as jnp
from jax import lax
from jax.experimental import pallas as pl
from jax.experimental.pallas import tpu as pltpu
from jax.sharding import PartitionSpec as P

BLOCK = 128
beta_one = 0.9
beta_two = 0.95
learn_rate = 0.01
decay_rate = 0.1
epsilon = 1e-08
scale_eps = 1e-05
correct_one = 1.0 - 0.9**10
correct_two = 1.0 - 0.95**10


def step(master, grad, moment, second):
    new_moment = beta_one * moment + (1.0 - beta_one) * grad
    new_second = beta_two * second + (1.0 - beta_two) * grad * grad
    update = (
        new_moment / correct_one / (jnp.sqrt(new_second / correct_two) + epsilon)
        + decay_rate * master
    )
    return master - learn_rate * update, new_moment, new_second


def scaled_block(new_master):
    scale = jnp.max(jnp.abs(new_master)) + scale_eps
    return new_master / scale, scale


def visit(n, first):
    rest = [k for k in range(n) if k != first]
    return [first] + sorted(rest, key=lambda k: (-min(abs(k - first), n - abs(k - first)), k))


def flip_kernel(order, master_ref, grad_ref, moment_ref, second_ref, own_ref):
    height, width = master_ref.shape
    rows = width // len(order)
    for j in range(width // BLOCK):
        cols = slice(j * BLOCK, (j + 1) * BLOCK)
        new_master, _, _ = step(master_ref[:, cols], grad_ref[:, cols], moment_ref[:, cols], second_ref[:, cols])
        scaled, _ = scaled_block(new_master)
        flipped = scaled.T.astype(jnp.bfloat16)
        for k, owner in enumerate(order):
            if owner * rows // BLOCK == j:
                at = owner * rows - j * BLOCK
                own_ref[k * rows : (k + 1) * rows, :] = flipped[at : at + rows]
        own_ref[width + j * height : width + (j + 1) * height, :] = scaled.astype(jnp.bfloat16)


def repeat_kernel(load_ref, copies_ref):
    for k in range(copies_ref.shape[0]):
        copies_ref[k] = load_ref[...]


def spread_kernel(order, load_ref, copies_ref):
    sides, slabs = load_ref.shape[:2]
    for side in range(sides):
        for s in range(slabs):
            for k, owner in enumerate(order):
                tile = load_ref[side, s, k]
                for n in range(copies_ref.shape[0]):
                    copies_ref[n, side, s, owner] = tile


def place_own(forward_order, flipped_order, flip, slabs_ref, forward_ref, flipped_ref, sem, work=None):
    core = (lax.axis_index("tensor") & 1) ^ flip
    width = forward_ref.shape[2] // slabs_ref.shape[0]

    def forward():
        copies = []
        for k, chip in enumerate(forward_order):
            for s in range(2):
                for j in range(width // BLOCK):
                    start = (2 * chip + s) * width + j * BLOCK
                    copies.append(
                        pltpu.make_async_copy(
                            slabs_ref.at[2 * k + s, j], forward_ref.at[:, :, start : start + BLOCK], sem
                        )
                    )
        return copies

    def flipped():
        copies = []
        for p, (chip, side) in enumerate(flipped_order):
            for s in range(2):
                copies.append(pltpu.make_async_copy(slabs_ref.at[p, s], flipped_ref.at[2 * chip + s, :, side], sem))
        return copies

    for which, copies in ((0, forward), (1, flipped)):

        @pl.when(core == which)
        def _(copies=copies):
            for copy in copies():
                copy.start()

    if work is not None:
        work()

    for which, copies in ((0, forward), (1, flipped)):

        @pl.when(core == which)
        def _(copies=copies):
            for copy in copies():
                copy.wait()


def finish_kernel(orders, slabs_ref, master_ref, grad_ref, moment_ref, second_ref, forward_ref, flipped_ref, out_master, out_moment, out_second, scale_ref, sem):
    def work():
        height, width = master_ref.shape
        for j in range(width // BLOCK):
            cols = slice(j * BLOCK, (j + 1) * BLOCK)
            new_master, new_moment, new_second = step(
                master_ref[:, cols], grad_ref[:, cols], moment_ref[:, cols], second_ref[:, cols]
            )
            out_master[:, cols] = new_master
            out_moment[:, cols] = new_moment
            out_second[:, cols] = new_second
            _, scale = scaled_block(new_master)
            scale_ref[0, j] = scale

    place_own(*orders, 0, slabs_ref, forward_ref, flipped_ref, sem, work)


def place_kernel(orders, slabs_ref, _, __, forward_ref, flipped_ref, sem):
    place_own(*orders, 1, slabs_ref, forward_ref, flipped_ref, sem)


def in_vmem(x):
    return pltpu.with_memory_space_constraint(x, pltpu.VMEM)


whole = pl.BlockSpec(memory_space=pltpu.VMEM)
hbm = pl.BlockSpec(memory_space=pl.ANY)


def body(master, grad, moment, second):
    height, width = master.shape
    n_dp, n_tensor = lax.axis_size("dp"), lax.axis_size("tensor")
    n_z, n_chip, n_side, tile = n_dp // 2, n_tensor // 2, 2, 8
    f32, bf16 = jnp.float32, jnp.bfloat16
    rows = height * width // BLOCK
    z_order = visit(n_z, n_z // 2)
    chip_order = visit(n_chip, n_chip // 2 + 1)
    plane_order = [(chip, side) for chip in chip_order for side in range(n_side)]
    orders = (chip_order, plane_order)
    own = pl.pallas_call(
        lambda *refs: flip_kernel(z_order, *refs),
        out_shape=pltpu.VMEM((2 * rows, BLOCK), bf16),
        in_specs=[whole] * 4,
        out_specs=whole,
        cost_estimate=pl.CostEstimate(flops=20 * height * width, bytes_accessed=16 * height * width, transcendentals=0),
        name="flip",
    )(master, grad, moment, second)
    both = lax.all_gather(own, "tensor", axis=0, axis_index_groups=[[2 * k, 2 * k + 1] for k in range(n_chip)])

    def forward_part(both):
        copies = pl.pallas_call(
            repeat_kernel,
            out_shape=pltpu.VMEM((n_chip, 2 * rows, BLOCK), bf16),
            in_specs=[whole],
            out_specs=whole,
            name="repeat",
        )(in_vmem(both[:, rows:].reshape(2 * rows, BLOCK)))
        groups = [[2 * k + c for k in chip_order] for c in range(2)]
        slabs = lax.all_to_all(copies, "tensor", 0, 0, tiled=True, axis_index_groups=groups)
        return slabs.reshape(n_tensor, width // BLOCK, height // tile, tile, BLOCK)

    def flipped_part(both):
        pieces = both[:, :rows].reshape(2, n_z, n_side, tile, BLOCK).transpose(1, 2, 0, 3, 4)
        groups = [[n_side * z + side for z in z_order] for side in range(n_side)]
        pieces = lax.all_to_all(pieces, "dp", 0, 0, tiled=True, axis_index_groups=groups)
        copies = pl.pallas_call(
            lambda *refs: spread_kernel(z_order, *refs),
            out_shape=pltpu.VMEM((n_chip, n_side, 2, n_z, tile, BLOCK), bf16),
            in_specs=[whole],
            out_specs=whole,
            name="spread",
        )(in_vmem(pieces.transpose(1, 2, 0, 3, 4)))
        groups = [
            [(n_side * z + side) * n_tensor + 2 * chip + c for chip, side in plane_order] for z in range(n_z) for c in range(2)
        ]
        slabs = lax.all_to_all(
            copies.reshape(n_chip * n_side, 2, n_z, tile, BLOCK), ("dp", "tensor"), 0, 0, tiled=True, axis_index_groups=groups
        )
        return slabs.reshape(n_tensor, width // BLOCK, height // tile, tile, BLOCK)

    mine = lax.cond(lax.axis_index("tensor") % 2 == 1, flipped_part, forward_part, both)
    other = lax.ppermute(mine, "tensor", [(i, i ^ 1) for i in range(n_tensor)])
    same = jax.ShapeDtypeStruct((height, width), f32)
    outs = (
        jax.ShapeDtypeStruct((height // tile, tile, n_tensor * width), bf16),
        jax.ShapeDtypeStruct((n_tensor, n_z, n_side, tile, BLOCK), bf16),
    )
    forward_copy, transposed_copy, new_master, new_moment, new_second, block_scales = pl.pallas_call(
        lambda *refs: finish_kernel(orders, *refs),
        out_shape=(*outs, same, same, same, jax.ShapeDtypeStruct((1, width // BLOCK), f32)),
        in_specs=[whole] * 5,
        out_specs=(hbm, hbm, whole, whole, whole, pl.BlockSpec(memory_space=pltpu.SMEM)),
        scratch_shapes=[pltpu.SemaphoreType.DMA],
        cost_estimate=pl.CostEstimate(flops=20 * height * width, bytes_accessed=4 * mine.size, transcendentals=0),
        name="finish",
    )(in_vmem(mine), *(in_vmem(x) for x in (master, grad, moment, second)))
    forward_copy, transposed_copy = pl.pallas_call(
        lambda *refs: place_kernel(orders, *refs),
        out_shape=outs,
        in_specs=[whole, hbm, hbm],
        out_specs=(hbm, hbm),
        scratch_shapes=[pltpu.SemaphoreType.DMA],
        input_output_aliases={1: 0, 2: 1},
        cost_estimate=pl.CostEstimate(flops=0, bytes_accessed=4 * mine.size, transcendentals=0),
        name="place",
    )(in_vmem(other), forward_copy, transposed_copy)
    forward_copy = forward_copy.reshape(height, n_tensor * width)
    transposed_copy = transposed_copy.reshape(n_tensor, n_dp, tile, BLOCK).transpose(0, 2, 1, 3).reshape(n_tensor, tile, n_dp * BLOCK)
    return (new_master, new_moment, new_second, block_scales, forward_copy, transposed_copy)


def solution(mesh):
    spec = P("dp", "tensor")
    return jax.shard_map(
        body,
        mesh=mesh,
        in_specs=(spec,) * 4,
        out_specs=(spec, spec, spec, spec, P("dp", None), P(None, "dp", None)),
        check_vma=False,
    )
```

time: 70.9 us -> 48.1 us (0.68)
  starting transfers between devices: 32.7 us -> 1.91 us
  blocking collectives: 15.2 us -> 40.1 us
  waiting for transfers between devices: 13.4 us -> 0.86 us
  local copies, waits for them, and re-layouts: 2.92 us -> 0.07 us
  other arithmetic: 1.24 us -> 0 us
    all_to_all x2 -> x0, starting transfers between devices: 20.5 us -> none  [the longest x1 17 us: body(): lax.all_to_all(flipped.reshape(n_dp, width // n_dp, height), 'dp', 0, 0,...]
    all_to_all x1 -> x2, blocking collectives: 15.2 us -> 31.5 us  [the longest x1 16.4 us: flipped_part(): lax.all_to_all(pieces, 'dp', 0, 0, tiled=True, axis_index_groups=groups)]
    all_to_all x2 -> x0, waiting for transfers between devices: 13.4 us -> none  [the longest x1 10.4 us: body(): lax.all_to_all(flipped.reshape(n_dp, width // n_dp, height), 'dp', 0, 0,...]
    ppermute x2 -> x1, starting transfers between devices: 12.2 us -> 1.91 us  [body(): other = lax.ppermute(mine, 'tensor', [(i, i ^ 1) for i in range(n_tensor)])]
    all_gather x0 -> x1, blocking collectives: none -> 8.51 us  [body(): lax.all_gather(own, 'tensor', axis=0, axis_index_groups=[[2 * k, 2 * k +...]
    unnamed x1 -> x8, local copies, waits for them, and re-layouts: 1.31 us -> 0.01 us
    select_n x2 -> x0, other arithmetic: 1.24 us -> none  [the longest x1 1.07 us: body(): jnp.where(first, jnp.stack([mine_t, other_t], 1), jnp.stack([other_t, min...]
    broadcast_in_dim x1 -> x0, local copies, waits for them, and re-layouts: 0.86 us -> none  [body(): jnp.broadcast_to(pieces[None], (half, *pieces.shape))]
  transfers between devices with their start and end apart: 4 -> 1, of which waited for: 2 -> 1; matrix products, arithmetic and copies ran while one was open for 3% -> 0% of each run, Pallas kernels for 3% -> 4%
where the time goes in v3:
time: 48.1 us; the launch traced here: 47.9 us
  blocking collectives  40.1 us (83%)
  Pallas kernels  4.25 us (9%)
  starting transfers between devices  1.91 us (4%)
  waiting for transfers between devices  0.86 us (2%)
  between operations  0.7 us (1%)
    all_to_all x1, blocking collectives, flipped_part(): lax.all_to_all(pieces, 'dp', 0, 0, tiled=True, axis_index_groups=groups)  16.4 us
    all_to_all x1, blocking collectives, flipped_part(): lax.all_to_all(copies.reshape(n_chip * n_side, 2, n_z, tile, BLOCK), ('dp...  15.2 us
    all_gather x1, blocking collectives, body(): lax.all_gather(own, 'tensor', axis=0, axis_index_groups=[[2 * k, 2 * k +...  8.51 us
    ppermute x1, starting transfers between devices, body(): other = lax.ppermute(mine, 'tensor', [(i, i ^ 1) for i in range(n_tensor)])  1.91 us
    pallas_call x1, Pallas kernels, body(): pl.pallas_call(lambda *refs: finish_kernel(orders, *refs), out_shape=(*ou...  1.72 us
    pallas_call x1, Pallas kernels, body(): pl.pallas_call(lambda *refs: flip_kernel(z_order, *refs), out_shape=pltpu...  1.43 us
  transfers between devices with their start and end apart: 1, of which 1 were waited for; matrix products, arithmetic and copies ran while one was open for 0% of the time, Pallas kernels for 4%

profile of v3, /device:TPU:1, one launch (start us, length us, event | category | flops | bytes accessed | tf_op | source)
XLA Modules:
  0.0 47.9 jit_solution(16225873405735755259)
XLA Ops:
  0.6 1.4 %flip.1 = bf16[512,128]{1,0:T(8,128)(2,1)S(1)} custom-call(f32[128,256]{1,0:T(8,128)} %refs_1_.3, f32[128,256]{1,0:T(8,128)} %refs_2_.3, f32[128,256]{1,0:T(8,128)} %refs_3_.3, f32[128,256]{1,0:T(8,128)} %refs_4_.1), custom_call_target="tpu_custom_call" | custom-call | flops 655360 | bytes 524288 | tf_op jit(solution)/shard_map/flip/pallas_call | solution.py:150
  2.1 8.5 %all-gather = bf16[1024,128]{1,0:T(8,128)(2,1)S(1)} all-gather(bf16[512,128]{1,0:T(8,128)(2,1)S(1)} %flip.1), channel_id=2, replica_groups={{0,1},{2,3},{4,5},{6,7},{8,9},{10,11},{12,13},{14,15},{16,17},{18,19},{..., dimensions={0}, use_global_device_ids=true | all-gather | bytes 393216 | tf_op jit(solution)/shard_map/all_gather | solution.py:158
  10.6 0.0 copy-start
  10.6 0.0 copy-start.1
  10.6 0.0 copy-start.2
  10.6 0.0 copy-start.3
  10.6 31.8 %conditional.1 = (bf16[16,2,16,8,128]{4,3,2,1,0:T(8,128)(2,1)S(1)}) conditional(s32[]{:T(128)} %convert_element_type.3, bf16[2,512,128]{2,1,0:T(8,128)(2,1)S(1)} %bitcast.22, bf16[2,512,128]{2,1,0:T(8,128)(2,1)S(1)} %bitcast.23), branch_computations={%region_0.1_spmd, %region_1.2_spmd} | conditional | bytes 3145736 | solution.py:191
  10.7 16.4 %all_to_all.13 = bf16[16,2,2,8,128]{4,3,2,1,0:T(8,128)(2,1)S(1)} all-to-all(bf16[16,2,2,8,128]{4,3,2,1,0:T(8,128)(2,1)S(1)} %copy.13), channel_id=1, replica_groups={{256,0,32,480,64,448,96,416,128,384,160,352,192,320,224,288},{272,16,48..., dimensions={0} | all-to-all | bytes 262144 | tf_op jit(solution)/shard_map/cond/branch_1_fun/all_to_all | solution.py:175
  27.1 0.1 spread.1
  27.2 15.2 %all_to_all.14 = bf16[16,2,16,8,128]{4,3,2,1,0:T(8,128)(2,1)S(1)} all-to-all(bf16[16,2,16,8,128]{4,3,2,1,0:T(8,128)(2,1)S(1)} %bitcast.17), channel_id=1, replica_groups={{10,26,2,18,0,16,4,20,6,22,14,30,8,24,12,28},{11,27,3,19,1,17,5,21,7,23..., dimensions={0} | all-to-all | bytes 2097152 | tf_op jit(solution)/shard_map/cond/branch_1_fun/all_to_all | solution.py:186
  42.4 1.9 %collective-permute-start = (bf16[16,2,16,8,128]{4,3,2,1,0:T(8,128)(2,1)S(1)}, bf16[16,2,16,8,128]{4,3,2,1,0:T(8,128)(2,1)S(1)}, u32[]{:S(2)}, u32[]{:S(2)}) collective-permute-start(bf16[16,2,16,8,128]{4,3,2,1,0:T(8,128)(2,1)S(1)} %get-tuple-element.27.refs_0_), channel_id=1, source_target_pairs={{0,1},{1,0},{2,3},{3,2},{4,5},{5,4},{6,7},{7,6},{8,9},{9,8},{10,11... | collective-permute-start | bytes 3145736 | tf_op jit(solution)/shard_map/ppermute | solution.py:192
  44.3 0.0 copy-done
  44.3 0.0 copy-done.1
  44.3 0.0 copy-done.2
  44.3 0.0 copy-done.3
  44.4 1.7 %finish.1 = (bf16[16,8,4096]{2,1,0:T(8,128)(2,1)}, bf16[16,16,2,8,128]{4,3,2,1,0:T(8,128)(2,1)}, f32[128,256]{1,0:T(8,128)}, f32[128,256]{1,0:T(8,128)}, f32[128,256]{1,0:T(8,128)}, /*index=5*/f32[1,2]{1,0:T(1,128)}) custom-call(bf16[16,2,16,8,128]{4,3,2,1,0:T(8,128)(2,1)S(1)} %get-tuple-element.27.refs_0_, f32[128,256]{1,0:T(8,128)S(1)} %copy-done, ...), custom_call_target="tpu_custom_call" | custom-call | flops 655360 | bytes 2097152 | tf_op jit(solution)/shard_map/finish/pallas_call | solution.py:198
  46.1 0.9 %collective-permute-done.refs_0_ = bf16[16,2,16,8,128]{4,3,2,1,0:T(8,128)(2,1)S(1)} collective-permute-done((bf16[16,2,16,8,128]{4,3,2,1,0:T(8,128)(2,1)S(1)}, bf16[16,2,16,8,128]{4,3,2,1,0:T(8,128)(2,1)S(1)}, u32[]{:S(2)}, u32[]{:S(2)}) %collective-permute-start) | collective-permute-done | bytes 1048608 | tf_op jit(solution)/shard_map/ppermute | solution.py:192
  46.9 0.9 %place.1 = (bf16[16,8,4096]{2,1,0:T(8,128)(2,1)}, bf16[16,16,2,8,128]{4,3,2,1,0:T(8,128)(2,1)}) custom-call(bf16[16,2,16,8,128]{4,3,2,1,0:T(8,128)(2,1)S(1)} %collective-permute-done.refs_0_, bf16[16,8,4096]{2,1,0:T(8,128)(2,1)} %get-tuple-element.23.refs_1_, ...), custom_call_target="tpu_custom_call", output_to_operand_aliasing={{0}: (1, {}), {1}: (2, {})} | custom-call | bytes 2097152 | tf_op jit(solution)/shard_map/place/pallas_call | solution.py:207
  (3 shorter events, 0.1 us)
Async XLA Ops:
  10.6 33.7 %copy-start = (f32[128,256]{1,0:T(8,128)S(1)}, f32[128,256]{1,0:T(8,128)}, u32[]{:S(2)}) copy-start(f32[128,256]{1,0:T(8,128)} %refs_1_.3) | copy-start | bytes 393220
  10.6 33.7 %copy-start.1 = (f32[128,256]{1,0:T(8,128)S(1)}, f32[128,256]{1,0:T(8,128)}, u32[]{:S(2)}) copy-start(f32[128,256]{1,0:T(8,128)} %refs_2_.3) | copy-start | bytes 393220
  10.6 33.7 %copy-start.2 = (f32[128,256]{1,0:T(8,128)S(1)}, f32[128,256]{1,0:T(8,128)}, u32[]{:S(2)}) copy-start(f32[128,256]{1,0:T(8,128)} %refs_3_.3) | copy-start | bytes 393220
  10.6 33.7 %copy-start.3 = (f32[128,256]{1,0:T(8,128)S(1)}, f32[128,256]{1,0:T(8,128)}, u32[]{:S(2)}) copy-start(f32[128,256]{1,0:T(8,128)} %refs_4_.1) | copy-start | bytes 393220
  42.4 4.5 %collective-permute-start = (bf16[16,2,16,8,128]{4,3,2,1,0:T(8,128)(2,1)S(1)}, bf16[16,2,16,8,128]{4,3,2,1,0:T(8,128)(2,1)S(1)}, u32[]{:S(2)}, u32[]{:S(2)}) collective-permute-start(bf16[16,2,16,8,128]{4,3,2,1,0:T(8,128)(2,1)S(1)} %get-tuple-element.27.refs_0_), channel_id=1, source_target_pairs={{0,1},{1,0},{2,3},{3,2},{4,5},{5,4},{6,7},{7,6},{8,9},{9,8},{10,11... | collective-permute-start | bytes 3145736 | tf_op jit(solution)/shard_map/ppermute | solution.py:192

commit v4 on v3

--- a/solution.py
+++ b/solution.py
@@ -31,9 +31,16 @@
     return new_master / scale, scale
 
 
-def visit(n, first):
-    rest = [k for k in range(n) if k != first]
-    return [first] + sorted(rest, key=lambda k: (-min(abs(k - first), n - abs(k - first)), k))
+def z_visit(n):
+    lead = n // 2 + 1
+    far = [k for k in (0, 8, 1, 10, 2, 7, 15, 11, 3, 6, 14, 12, 4, 5, 13) if k < n and k != lead]
+    rest = [k for k in range(n) if k != lead and k not in far]
+    return [lead] + far + rest
+
+
+def plane_visit(nx, ny, n_side):
+    pairs = [((nx // 2 - i) % nx, (ny // 2 - j) % ny) for j in range(ny) for i in range(nx)]
+    return [(x * (ny // n_side) + y // n_side, y % n_side) for x, y in pairs]
 
 
 def flip_kernel(order, master_ref, grad_ref, moment_ref, second_ref, own_ref):
@@ -56,14 +63,15 @@
         copies_ref[k] = load_ref[...]
 
 
-def spread_kernel(order, load_ref, copies_ref):
+def spread_kernel(z_order, plane_order, load_ref, copies_ref):
     sides, slabs = load_ref.shape[:2]
     for side in range(sides):
         for s in range(slabs):
-            for k, owner in enumerate(order):
+            for k, owner in enumerate(z_order):
                 tile = load_ref[side, s, k]
-                for n in range(copies_ref.shape[0]):
-                    copies_ref[n, side, s, owner] = tile
+                for n, (_, its) in enumerate(plane_order):
+                    if its == side:
+                        copies_ref[n, s, owner] = tile
 
 
 def place_own(forward_order, flipped_order, flip, slabs_ref, forward_ref, flipped_ref, sem, work=None):
@@ -94,8 +102,8 @@
 
         @pl.when(core == which)
         def _(copies=copies):
-            for copy in copies():
-                copy.start()
+            for n, copy in enumerate(copies()):
+                copy.start(priority=n % 2)
 
     if work is not None:
         work()
@@ -143,9 +151,9 @@
     n_z, n_chip, n_side, tile = n_dp // 2, n_tensor // 2, 2, 8
     f32, bf16 = jnp.float32, jnp.bfloat16
     rows = height * width // BLOCK
-    z_order = visit(n_z, n_z // 2)
-    chip_order = visit(n_chip, n_chip // 2 + 1)
-    plane_order = [(chip, side) for chip in chip_order for side in range(n_side)]
+    z_order = z_visit(n_z)
+    chip_order = [(n_chip // 2 + 1 + k) % n_chip for k in range(n_chip)]
+    plane_order = plane_visit(4, n_chip // 4 * n_side, n_side)
     orders = (chip_order, plane_order)
     own = pl.pallas_call(
         lambda *refs: flip_kernel(z_order, *refs),
@@ -174,8 +182,8 @@
         groups = [[n_side * z + side for z in z_order] for side in range(n_side)]
         pieces = lax.all_to_all(pieces, "dp", 0, 0, tiled=True, axis_index_groups=groups)
         copies = pl.pallas_call(
-            lambda *refs: spread_kernel(z_order, *refs),
-            out_shape=pltpu.VMEM((n_chip, n_side, 2, n_z, tile, BLOCK), bf16),
+            lambda *refs: spread_kernel(z_order, plane_order, *refs),
+            out_shape=pltpu.VMEM((n_tensor, 2, n_z, tile, BLOCK), bf16),
             in_specs=[whole],
             out_specs=whole,
             name="spread",
@@ -184,7 +192,7 @@
             [(n_side * z + side) * n_tensor + 2 * chip + c for chip, side in plane_order] for z in range(n_z) for c in range(2)
         ]
         slabs = lax.all_to_all(
-            copies.reshape(n_chip * n_side, 2, n_z, tile, BLOCK), ("dp", "tensor"), 0, 0, tiled=True, axis_index_groups=groups
+            copies, ("dp", "tensor"), 0, 0, tiled=True, axis_index_groups=groups
         )
         return slabs.reshape(n_tensor, width // BLOCK, height // tile, tile, BLOCK)
 

time: 48.1 us -> 47.8 us (level)
  no operation moved by 1% of the time
where the time goes in v4:
time: 47.8 us; the launch traced here: 47.6 us
  blocking collectives  39.7 us (83%)
  Pallas kernels  4.28 us (9%)
  starting transfers between devices  1.91 us (4%)
  waiting for transfers between devices  0.86 us (2%)
  between operations  0.7 us (1%)
    all_to_all x1, blocking collectives, flipped_part(): lax.all_to_all(pieces, 'dp', 0, 0, tiled=True, axis_index_groups=groups)  16 us
    all_to_all x1, blocking collectives, flipped_part(): lax.all_to_all(copies, ('dp', 'tensor'), 0, 0, tiled=True, axis_index_gro...  15.2 us
    all_gather x1, blocking collectives, body(): lax.all_gather(own, 'tensor', axis=0, axis_index_groups=[[2 * k, 2 * k +...  8.51 us
    ppermute x1, starting transfers between devices, body(): other = lax.ppermute(mine, 'tensor', [(i, i ^ 1) for i in range(n_tensor)])  1.91 us
    pallas_call x1, Pallas kernels, body(): pl.pallas_call(lambda *refs: finish_kernel(orders, *refs), out_shape=(*ou...  1.72 us
    pallas_call x1, Pallas kernels, body(): pl.pallas_call(lambda *refs: flip_kernel(z_order, *refs), out_shape=pltpu...  1.43 us
  transfers between devices with their start and end apart: 1, of which 1 were waited for; matrix products, arithmetic and copies ran while one was open for 0% of the time, Pallas kernels for 4%

profile of v4, /device:TPU:1, one launch (start us, length us, event | category | flops | bytes accessed | tf_op | source)
XLA Modules:
  0.0 47.6 jit_solution(8816258261965529245)
XLA Ops:
  0.6 1.4 %flip.1 = bf16[512,128]{1,0:T(8,128)(2,1)S(1)} custom-call(f32[128,256]{1,0:T(8,128)} %refs_1_.3, f32[128,256]{1,0:T(8,128)} %refs_2_.3, f32[128,256]{1,0:T(8,128)} %refs_3_.3, f32[128,256]{1,0:T(8,128)} %refs_4_.1), custom_call_target="tpu_custom_call" | custom-call | flops 655360 | bytes 524288 | tf_op jit(solution)/shard_map/flip/pallas_call | solution.py:158
  2.1 8.5 %all-gather = bf16[1024,128]{1,0:T(8,128)(2,1)S(1)} all-gather(bf16[512,128]{1,0:T(8,128)(2,1)S(1)} %flip.1), channel_id=2, replica_groups={{0,1},{2,3},{4,5},{6,7},{8,9},{10,11},{12,13},{14,15},{16,17},{18,19},{..., dimensions={0}, use_global_device_ids=true | all-gather | bytes 393216 | tf_op jit(solution)/shard_map/all_gather | solution.py:166
  10.6 0.0 copy-start
  10.6 0.0 copy-start.1
  10.6 0.0 copy-start.2
  10.6 0.0 copy-start.3
  10.6 31.5 %conditional.1 = (bf16[16,2,16,8,128]{4,3,2,1,0:T(8,128)(2,1)S(1)}) conditional(s32[]{:T(128)} %convert_element_type.3, bf16[2,512,128]{2,1,0:T(8,128)(2,1)S(1)} %bitcast.20, bf16[2,512,128]{2,1,0:T(8,128)(2,1)S(1)} %bitcast.21), branch_computations={%region_0.1_spmd, %region_1.2_spmd} | conditional | bytes 3145736 | solution.py:199
  10.7 16.0 %all_to_all.13 = bf16[16,2,2,8,128]{4,3,2,1,0:T(8,128)(2,1)S(1)} all-to-all(bf16[16,2,2,8,128]{4,3,2,1,0:T(8,128)(2,1)S(1)} %copy.13), channel_id=1, replica_groups={{288,0,256,32,320,64,224,480,352,96,192,448,384,128,160,416},{304,16,27..., dimensions={0} | all-to-all | bytes 262144 | tf_op jit(solution)/shard_map/cond/branch_1_fun/all_to_all | solution.py:183
  26.7 0.2 spread.1
  26.9 15.2 %all_to_all.14 = bf16[16,2,16,8,128]{4,3,2,1,0:T(8,128)(2,1)S(1)} all-to-all(bf16[16,2,16,8,128]{4,3,2,1,0:T(8,128)(2,1)S(1)} %spread.1), channel_id=1, replica_groups={{10,6,2,14,24,20,16,28,8,4,0,12,26,22,18,30},{11,7,3,15,25,21,17,29,9,5..., dimensions={0} | all-to-all | bytes 2097152 | tf_op jit(solution)/shard_map/cond/branch_1_fun/all_to_all | solution.py:194
  42.1 1.9 %collective-permute-start = (bf16[16,2,16,8,128]{4,3,2,1,0:T(8,128)(2,1)S(1)}, bf16[16,2,16,8,128]{4,3,2,1,0:T(8,128)(2,1)S(1)}, u32[]{:S(2)}, u32[]{:S(2)}) collective-permute-start(bf16[16,2,16,8,128]{4,3,2,1,0:T(8,128)(2,1)S(1)} %get-tuple-element.27.refs_0_), channel_id=1, source_target_pairs={{0,1},{1,0},{2,3},{3,2},{4,5},{5,4},{6,7},{7,6},{8,9},{9,8},{10,11... | collective-permute-start | bytes 3145736 | tf_op jit(solution)/shard_map/ppermute | solution.py:200
  44.0 0.0 copy-done
  44.0 0.0 copy-done.1
  44.0 0.0 copy-done.2
  44.1 0.0 copy-done.3
  44.1 1.7 %finish.1 = (bf16[16,8,4096]{2,1,0:T(8,128)(2,1)}, bf16[16,16,2,8,128]{4,3,2,1,0:T(8,128)(2,1)}, f32[128,256]{1,0:T(8,128)}, f32[128,256]{1,0:T(8,128)}, f32[128,256]{1,0:T(8,128)}, /*index=5*/f32[1,2]{1,0:T(1,128)}) custom-call(bf16[16,2,16,8,128]{4,3,2,1,0:T(8,128)(2,1)S(1)} %get-tuple-element.27.refs_0_, f32[128,256]{1,0:T(8,128)S(1)} %copy-done, ...), custom_call_target="tpu_custom_call" | custom-call | flops 655360 | bytes 2097152 | tf_op jit(solution)/shard_map/finish/pallas_call | solution.py:206
  45.8 0.9 %collective-permute-done.refs_0_ = bf16[16,2,16,8,128]{4,3,2,1,0:T(8,128)(2,1)S(1)} collective-permute-done((bf16[16,2,16,8,128]{4,3,2,1,0:T(8,128)(2,1)S(1)}, bf16[16,2,16,8,128]{4,3,2,1,0:T(8,128)(2,1)S(1)}, u32[]{:S(2)}, u32[]{:S(2)}) %collective-permute-start) | collective-permute-done | bytes 1048608 | tf_op jit(solution)/shard_map/ppermute | solution.py:200
  46.6 0.9 %place.1 = (bf16[16,8,4096]{2,1,0:T(8,128)(2,1)}, bf16[16,16,2,8,128]{4,3,2,1,0:T(8,128)(2,1)}) custom-call(bf16[16,2,16,8,128]{4,3,2,1,0:T(8,128)(2,1)S(1)} %collective-permute-done.refs_0_, bf16[16,8,4096]{2,1,0:T(8,128)(2,1)} %get-tuple-element.23.refs_1_, ...), custom_call_target="tpu_custom_call", output_to_operand_aliasing={{0}: (1, {}), {1}: (2, {})} | custom-call | bytes 2097152 | tf_op jit(solution)/shard_map/place/pallas_call | solution.py:215
  (3 shorter events, 0.1 us)
Async XLA Ops:
  10.6 33.4 %copy-start = (f32[128,256]{1,0:T(8,128)S(1)}, f32[128,256]{1,0:T(8,128)}, u32[]{:S(2)}) copy-start(f32[128,256]{1,0:T(8,128)} %refs_1_.3) | copy-start | bytes 393220
  10.6 33.4 %copy-start.1 = (f32[128,256]{1,0:T(8,128)S(1)}, f32[128,256]{1,0:T(8,128)}, u32[]{:S(2)}) copy-start(f32[128,256]{1,0:T(8,128)} %refs_2_.3) | copy-start | bytes 393220
  10.6 33.4 %copy-start.2 = (f32[128,256]{1,0:T(8,128)S(1)}, f32[128,256]{1,0:T(8,128)}, u32[]{:S(2)}) copy-start(f32[128,256]{1,0:T(8,128)} %refs_3_.3) | copy-start | bytes 393220
  10.6 33.5 %copy-start.3 = (f32[128,256]{1,0:T(8,128)S(1)}, f32[128,256]{1,0:T(8,128)}, u32[]{:S(2)}) copy-start(f32[128,256]{1,0:T(8,128)} %refs_4_.1) | copy-start | bytes 393220
  42.1 4.5 %collective-permute-start = (bf16[16,2,16,8,128]{4,3,2,1,0:T(8,128)(2,1)S(1)}, bf16[16,2,16,8,128]{4,3,2,1,0:T(8,128)(2,1)S(1)}, u32[]{:S(2)}, u32[]{:S(2)}) collective-permute-start(bf16[16,2,16,8,128]{4,3,2,1,0:T(8,128)(2,1)S(1)} %get-tuple-element.27.refs_0_), channel_id=1, source_target_pairs={{0,1},{1,0},{2,3},{3,2},{4,5},{5,4},{6,7},{7,6},{8,9},{9,8},{10,11... | collective-permute-start | bytes 3145736 | tf_op jit(solution)/shard_map/ppermute | solution.py:200

commit v5 on v4

--- a/solution.py
+++ b/solution.py
@@ -43,8 +43,19 @@
     return [(x * (ny // n_side) + y // n_side, y % n_side) for x, y in pairs]
 
 
-def flip_kernel(order, master_ref, grad_ref, moment_ref, second_ref, own_ref):
-    height, width = master_ref.shape
+def flip_kernel(order, master_hbm, grad_hbm, moment_hbm, second_hbm, own_ref, held, sem):
+    part = master_hbm.shape[0] // 4
+    copies = [
+        pltpu.make_async_copy(ref.at[pl.ds(k * part, part)], held.at[n, pl.ds(k * part, part)], sem)
+        for k in range(4)
+        for n, ref in enumerate((master_hbm, grad_hbm, moment_hbm, second_hbm))
+    ]
+    for n, copy in enumerate(copies):
+        copy.start(priority=n % 2)
+    for copy in copies:
+        copy.wait()
+    master_ref, grad_ref, moment_ref, second_ref = (held.at[n] for n in range(4))
+    height, width = master_hbm.shape
     rows = width // len(order)
     for j in range(width // BLOCK):
         cols = slice(j * BLOCK, (j + 1) * BLOCK)
@@ -158,8 +169,9 @@
     own = pl.pallas_call(
         lambda *refs: flip_kernel(z_order, *refs),
         out_shape=pltpu.VMEM((2 * rows, BLOCK), bf16),
-        in_specs=[whole] * 4,
+        in_specs=[hbm] * 4,
         out_specs=whole,
+        scratch_shapes=[pltpu.VMEM((4, height, width), f32), pltpu.SemaphoreType.DMA],
         cost_estimate=pl.CostEstimate(flops=20 * height * width, bytes_accessed=16 * height * width, transcendentals=0),
         name="flip",
     )(master, grad, moment, second)

time: 47.8 us -> 47.8 us (level)
  no operation moved by 1% of the time
where the time goes in v5:
time: 47.8 us; the launch traced here: 47.5 us
  blocking collectives  39.7 us (83%)
  Pallas kernels  4.2 us (9%)
  starting transfers between devices  1.91 us (4%)
  waiting for transfers between devices  0.86 us (2%)
  between operations  0.7 us (1%)
    all_to_all x1, blocking collectives, flipped_part(): lax.all_to_all(pieces, 'dp', 0, 0, tiled=True, axis_index_groups=groups)  16 us
    all_to_all x1, blocking collectives, flipped_part(): lax.all_to_all(copies, ('dp', 'tensor'), 0, 0, tiled=True, axis_index_gro...  15.2 us
    all_gather x1, blocking collectives, body(): lax.all_gather(own, 'tensor', axis=0, axis_index_groups=[[2 * k, 2 * k +...  8.51 us
    ppermute x1, starting transfers between devices, body(): other = lax.ppermute(mine, 'tensor', [(i, i ^ 1) for i in range(n_tensor)])  1.91 us
    pallas_call x1, Pallas kernels, body(): pl.pallas_call(lambda *refs: finish_kernel(orders, *refs), out_shape=(*ou...  1.72 us
    pallas_call x1, Pallas kernels, body(): pl.pallas_call(lambda *refs: flip_kernel(z_order, *refs), out_shape=pltpu...  1.35 us
  transfers between devices with their start and end apart: 1, of which 1 were waited for; matrix products, arithmetic and copies ran while one was open for 0% of the time, Pallas kernels for 4%

profile of v5, /device:TPU:1, one launch (start us, length us, event | category | flops | bytes accessed | tf_op | source)
XLA Modules:
  0.0 47.5 jit_solution(499826442178643016)
XLA Ops:
  0.6 1.3 %flip.1 = bf16[512,128]{1,0:T(8,128)(2,1)S(1)} custom-call(f32[128,256]{1,0:T(8,128)} %refs_1_.3, f32[128,256]{1,0:T(8,128)} %refs_2_.3, f32[128,256]{1,0:T(8,128)} %refs_3_.3, f32[128,256]{1,0:T(8,128)} %refs_4_.1), custom_call_target="tpu_custom_call" | custom-call | flops 655360 | bytes 524288 | tf_op jit(solution)/shard_map/flip/pallas_call | solution.py:169
  2.0 8.5 %all-gather = bf16[1024,128]{1,0:T(8,128)(2,1)S(1)} all-gather(bf16[512,128]{1,0:T(8,128)(2,1)S(1)} %flip.1), channel_id=2, replica_groups={{0,1},{2,3},{4,5},{6,7},{8,9},{10,11},{12,13},{14,15},{16,17},{18,19},{..., dimensions={0}, use_global_device_ids=true | all-gather | bytes 393216 | tf_op jit(solution)/shard_map/all_gather | solution.py:178
  10.5 0.0 copy-start
  10.5 0.0 copy-start.1
  10.5 0.0 copy-start.2
  10.5 0.0 copy-start.3
  10.5 31.5 %conditional.1 = (bf16[16,2,16,8,128]{4,3,2,1,0:T(8,128)(2,1)S(1)}) conditional(s32[]{:T(128)} %convert_element_type.3, bf16[2,512,128]{2,1,0:T(8,128)(2,1)S(1)} %bitcast.20, bf16[2,512,128]{2,1,0:T(8,128)(2,1)S(1)} %bitcast.21), branch_computations={%region_0.1_spmd, %region_1.2_spmd} | conditional | bytes 3145736 | solution.py:211
  10.6 16.0 %all_to_all.13 = bf16[16,2,2,8,128]{4,3,2,1,0:T(8,128)(2,1)S(1)} all-to-all(bf16[16,2,2,8,128]{4,3,2,1,0:T(8,128)(2,1)S(1)} %copy.13), channel_id=1, replica_groups={{288,0,256,32,320,64,224,480,352,96,192,448,384,128,160,416},{304,16,27..., dimensions={0} | all-to-all | bytes 262144 | tf_op jit(solution)/shard_map/cond/branch_1_fun/all_to_all | solution.py:195
  26.6 0.2 spread.1
  26.8 15.2 %all_to_all.14 = bf16[16,2,16,8,128]{4,3,2,1,0:T(8,128)(2,1)S(1)} all-to-all(bf16[16,2,16,8,128]{4,3,2,1,0:T(8,128)(2,1)S(1)} %spread.1), channel_id=1, replica_groups={{10,6,2,14,24,20,16,28,8,4,0,12,26,22,18,30},{11,7,3,15,25,21,17,29,9,5..., dimensions={0} | all-to-all | bytes 2097152 | tf_op jit(solution)/shard_map/cond/branch_1_fun/all_to_all | solution.py:206
  42.0 1.9 %collective-permute-start = (bf16[16,2,16,8,128]{4,3,2,1,0:T(8,128)(2,1)S(1)}, bf16[16,2,16,8,128]{4,3,2,1,0:T(8,128)(2,1)S(1)}, u32[]{:S(2)}, u32[]{:S(2)}) collective-permute-start(bf16[16,2,16,8,128]{4,3,2,1,0:T(8,128)(2,1)S(1)} %get-tuple-element.27.refs_0_), channel_id=1, source_target_pairs={{0,1},{1,0},{2,3},{3,2},{4,5},{5,4},{6,7},{7,6},{8,9},{9,8},{10,11... | collective-permute-start | bytes 3145736 | tf_op jit(solution)/shard_map/ppermute | solution.py:212
  43.9 0.0 copy-done
  43.9 0.0 copy-done.1
  44.0 0.0 copy-done.2
  44.0 0.0 copy-done.3
  44.0 1.7 %finish.1 = (bf16[16,8,4096]{2,1,0:T(8,128)(2,1)}, bf16[16,16,2,8,128]{4,3,2,1,0:T(8,128)(2,1)}, f32[128,256]{1,0:T(8,128)}, f32[128,256]{1,0:T(8,128)}, f32[128,256]{1,0:T(8,128)}, /*index=5*/f32[1,2]{1,0:T(1,128)}) custom-call(bf16[16,2,16,8,128]{4,3,2,1,0:T(8,128)(2,1)S(1)} %get-tuple-element.27.refs_0_, f32[128,256]{1,0:T(8,128)S(1)} %copy-done, ...), custom_call_target="tpu_custom_call" | custom-call | flops 655360 | bytes 2097152 | tf_op jit(solution)/shard_map/finish/pallas_call | solution.py:218
  45.7 0.9 %collective-permute-done.refs_0_ = bf16[16,2,16,8,128]{4,3,2,1,0:T(8,128)(2,1)S(1)} collective-permute-done((bf16[16,2,16,8,128]{4,3,2,1,0:T(8,128)(2,1)S(1)}, bf16[16,2,16,8,128]{4,3,2,1,0:T(8,128)(2,1)S(1)}, u32[]{:S(2)}, u32[]{:S(2)}) %collective-permute-start) | collective-permute-done | bytes 1048608 | tf_op jit(solution)/shard_map/ppermute | solution.py:212
  46.6 0.9 %place.1 = (bf16[16,8,4096]{2,1,0:T(8,128)(2,1)}, bf16[16,16,2,8,128]{4,3,2,1,0:T(8,128)(2,1)}) custom-call(bf16[16,2,16,8,128]{4,3,2,1,0:T(8,128)(2,1)S(1)} %collective-permute-done.refs_0_, bf16[16,8,4096]{2,1,0:T(8,128)(2,1)} %get-tuple-element.23.refs_1_, ...), custom_call_target="tpu_custom_call", output_to_operand_aliasing={{0}: (1, {}), {1}: (2, {})} | custom-call | bytes 2097152 | tf_op jit(solution)/shard_map/place/pallas_call | solution.py:227
  (3 shorter events, 0.1 us)
Async XLA Ops:
  10.5 33.4 %copy-start = (f32[128,256]{1,0:T(8,128)S(1)}, f32[128,256]{1,0:T(8,128)}, u32[]{:S(2)}) copy-start(f32[128,256]{1,0:T(8,128)} %refs_1_.3) | copy-start | bytes 393220
  10.5 33.4 %copy-start.1 = (f32[128,256]{1,0:T(8,128)S(1)}, f32[128,256]{1,0:T(8,128)}, u32[]{:S(2)}) copy-start(f32[128,256]{1,0:T(8,128)} %refs_2_.3) | copy-start | bytes 393220
  10.5 33.4 %copy-start.2 = (f32[128,256]{1,0:T(8,128)S(1)}, f32[128,256]{1,0:T(8,128)}, u32[]{:S(2)}) copy-start(f32[128,256]{1,0:T(8,128)} %refs_3_.3) | copy-start | bytes 393220
  10.5 33.5 %copy-start.3 = (f32[128,256]{1,0:T(8,128)S(1)}, f32[128,256]{1,0:T(8,128)}, u32[]{:S(2)}) copy-start(f32[128,256]{1,0:T(8,128)} %refs_4_.1) | copy-start | bytes 393220
  42.0 4.5 %collective-permute-start = (bf16[16,2,16,8,128]{4,3,2,1,0:T(8,128)(2,1)S(1)}, bf16[16,2,16,8,128]{4,3,2,1,0:T(8,128)(2,1)S(1)}, u32[]{:S(2)}, u32[]{:S(2)}) collective-permute-start(bf16[16,2,16,8,128]{4,3,2,1,0:T(8,128)(2,1)S(1)} %get-tuple-element.27.refs_0_), channel_id=1, source_target_pairs={{0,1},{1,0},{2,3},{3,2},{4,5},{5,4},{6,7},{7,6},{8,9},{9,8},{10,11... | collective-permute-start | bytes 3145736 | tf_op jit(solution)/shard_map/ppermute | solution.py:212

commit v6 on v5

--- a/solution.py
+++ b/solution.py
@@ -33,7 +33,7 @@
 
 def z_visit(n):
     lead = n // 2 + 1
-    far = [k for k in (0, 8, 1, 10, 2, 7, 15, 11, 3, 6, 14, 12, 4, 5, 13) if k < n and k != lead]
+    far = [k for k in (0, 8, 2, 10, 1, 7, 15, 11, 3, 6, 14, 12, 4, 5, 13) if k < n and k != lead]
     rest = [k for k in range(n) if k != lead and k not in far]
     return [lead] + far + rest
 

time: 47.8 us -> 47.8 us (level)
  no operation moved by 1% of the time
where the time goes in v6:
time: 47.8 us; the launch traced here: 47.5 us
  blocking collectives  39.7 us (83%)
  Pallas kernels  4.2 us (9%)
  starting transfers between devices  1.91 us (4%)
  waiting for transfers between devices  0.86 us (2%)
  between operations  0.7 us (1%)
    all_to_all x1, blocking collectives, flipped_part(): lax.all_to_all(pieces, 'dp', 0, 0, tiled=True, axis_index_groups=groups)  16 us
    all_to_all x1, blocking collectives, flipped_part(): lax.all_to_all(copies, ('dp', 'tensor'), 0, 0, tiled=True, axis_index_gro...  15.2 us
    all_gather x1, blocking collectives, body(): lax.all_gather(own, 'tensor', axis=0, axis_index_groups=[[2 * k, 2 * k +...  8.51 us
    ppermute x1, starting transfers between devices, body(): other = lax.ppermute(mine, 'tensor', [(i, i ^ 1) for i in range(n_tensor)])  1.91 us
    pallas_call x1, Pallas kernels, body(): pl.pallas_call(lambda *refs: finish_kernel(orders, *refs), out_shape=(*ou...  1.72 us
    pallas_call x1, Pallas kernels, body(): pl.pallas_call(lambda *refs: flip_kernel(z_order, *refs), out_shape=pltpu...  1.35 us
  transfers between devices with their start and end apart: 1, of which 1 were waited for; matrix products, arithmetic and copies ran while one was open for 0% of the time, Pallas kernels for 4%

profile of v6, /device:TPU:1, one launch (start us, length us, event | category | flops | bytes accessed | tf_op | source)
XLA Modules:
  0.0 47.5 jit_solution(1961990615828391279)
XLA Ops:
  0.6 1.3 %flip.1 = bf16[512,128]{1,0:T(8,128)(2,1)S(1)} custom-call(f32[128,256]{1,0:T(8,128)} %refs_1_.3, f32[128,256]{1,0:T(8,128)} %refs_2_.3, f32[128,256]{1,0:T(8,128)} %refs_3_.3, f32[128,256]{1,0:T(8,128)} %refs_4_.1), custom_call_target="tpu_custom_call" | custom-call | flops 655360 | bytes 524288 | tf_op jit(solution)/shard_map/flip/pallas_call | solution.py:169
  2.0 8.5 %all-gather = bf16[1024,128]{1,0:T(8,128)(2,1)S(1)} all-gather(bf16[512,128]{1,0:T(8,128)(2,1)S(1)} %flip.1), channel_id=2, replica_groups={{0,1},{2,3},{4,5},{6,7},{8,9},{10,11},{12,13},{14,15},{16,17},{18,19},{..., dimensions={0}, use_global_device_ids=true | all-gather | bytes 393216 | tf_op jit(solution)/shard_map/all_gather | solution.py:178
  10.5 0.0 copy-start
  10.5 0.0 copy-start.1
  10.5 0.0 copy-start.2
  10.5 0.0 copy-start.3
  10.5 31.5 %conditional.1 = (bf16[16,2,16,8,128]{4,3,2,1,0:T(8,128)(2,1)S(1)}) conditional(s32[]{:T(128)} %convert_element_type.3, bf16[2,512,128]{2,1,0:T(8,128)(2,1)S(1)} %bitcast.20, bf16[2,512,128]{2,1,0:T(8,128)(2,1)S(1)} %bitcast.21), branch_computations={%region_0.1_spmd, %region_1.2_spmd} | conditional | bytes 3145736 | solution.py:211
  10.6 16.0 %all_to_all.13 = bf16[16,2,2,8,128]{4,3,2,1,0:T(8,128)(2,1)S(1)} all-to-all(bf16[16,2,2,8,128]{4,3,2,1,0:T(8,128)(2,1)S(1)} %copy.13), channel_id=1, replica_groups={{288,0,256,64,320,32,224,480,352,96,192,448,384,128,160,416},{304,16,27..., dimensions={0} | all-to-all | bytes 262144 | tf_op jit(solution)/shard_map/cond/branch_1_fun/all_to_all | solution.py:195
  26.6 0.2 spread.1
  26.8 15.2 %all_to_all.14 = bf16[16,2,16,8,128]{4,3,2,1,0:T(8,128)(2,1)S(1)} all-to-all(bf16[16,2,16,8,128]{4,3,2,1,0:T(8,128)(2,1)S(1)} %spread.1), channel_id=1, replica_groups={{10,6,2,14,24,20,16,28,8,4,0,12,26,22,18,30},{11,7,3,15,25,21,17,29,9,5..., dimensions={0} | all-to-all | bytes 2097152 | tf_op jit(solution)/shard_map/cond/branch_1_fun/all_to_all | solution.py:206
  42.0 1.9 %collective-permute-start = (bf16[16,2,16,8,128]{4,3,2,1,0:T(8,128)(2,1)S(1)}, bf16[16,2,16,8,128]{4,3,2,1,0:T(8,128)(2,1)S(1)}, u32[]{:S(2)}, u32[]{:S(2)}) collective-permute-start(bf16[16,2,16,8,128]{4,3,2,1,0:T(8,128)(2,1)S(1)} %get-tuple-element.27.refs_0_), channel_id=1, source_target_pairs={{0,1},{1,0},{2,3},{3,2},{4,5},{5,4},{6,7},{7,6},{8,9},{9,8},{10,11... | collective-permute-start | bytes 3145736 | tf_op jit(solution)/shard_map/ppermute | solution.py:212
  43.9 0.0 copy-done
  43.9 0.0 copy-done.1
  44.0 0.0 copy-done.2
  44.0 0.0 copy-done.3
  44.0 1.7 %finish.1 = (bf16[16,8,4096]{2,1,0:T(8,128)(2,1)}, bf16[16,16,2,8,128]{4,3,2,1,0:T(8,128)(2,1)}, f32[128,256]{1,0:T(8,128)}, f32[128,256]{1,0:T(8,128)}, f32[128,256]{1,0:T(8,128)}, /*index=5*/f32[1,2]{1,0:T(1,128)}) custom-call(bf16[16,2,16,8,128]{4,3,2,1,0:T(8,128)(2,1)S(1)} %get-tuple-element.27.refs_0_, f32[128,256]{1,0:T(8,128)S(1)} %copy-done, ...), custom_call_target="tpu_custom_call" | custom-call | flops 655360 | bytes 2097152 | tf_op jit(solution)/shard_map/finish/pallas_call | solution.py:218
  45.7 0.9 %collective-permute-done.refs_0_ = bf16[16,2,16,8,128]{4,3,2,1,0:T(8,128)(2,1)S(1)} collective-permute-done((bf16[16,2,16,8,128]{4,3,2,1,0:T(8,128)(2,1)S(1)}, bf16[16,2,16,8,128]{4,3,2,1,0:T(8,128)(2,1)S(1)}, u32[]{:S(2)}, u32[]{:S(2)}) %collective-permute-start) | collective-permute-done | bytes 1048608 | tf_op jit(solution)/shard_map/ppermute | solution.py:212
  46.6 0.9 %place.1 = (bf16[16,8,4096]{2,1,0:T(8,128)(2,1)}, bf16[16,16,2,8,128]{4,3,2,1,0:T(8,128)(2,1)}) custom-call(bf16[16,2,16,8,128]{4,3,2,1,0:T(8,128)(2,1)S(1)} %collective-permute-done.refs_0_, bf16[16,8,4096]{2,1,0:T(8,128)(2,1)} %get-tuple-element.23.refs_1_, ...), custom_call_target="tpu_custom_call", output_to_operand_aliasing={{0}: (1, {}), {1}: (2, {})} | custom-call | bytes 2097152 | tf_op jit(solution)/shard_map/place/pallas_call | solution.py:227
  (3 shorter events, 0.1 us)
Async XLA Ops:
  10.5 33.4 %copy-start = (f32[128,256]{1,0:T(8,128)S(1)}, f32[128,256]{1,0:T(8,128)}, u32[]{:S(2)}) copy-start(f32[128,256]{1,0:T(8,128)} %refs_1_.3) | copy-start | bytes 393220
  10.5 33.4 %copy-start.1 = (f32[128,256]{1,0:T(8,128)S(1)}, f32[128,256]{1,0:T(8,128)}, u32[]{:S(2)}) copy-start(f32[128,256]{1,0:T(8,128)} %refs_2_.3) | copy-start | bytes 393220
  10.5 33.4 %copy-start.2 = (f32[128,256]{1,0:T(8,128)S(1)}, f32[128,256]{1,0:T(8,128)}, u32[]{:S(2)}) copy-start(f32[128,256]{1,0:T(8,128)} %refs_3_.3) | copy-start | bytes 393220
  10.5 33.5 %copy-start.3 = (f32[128,256]{1,0:T(8,128)S(1)}, f32[128,256]{1,0:T(8,128)}, u32[]{:S(2)}) copy-start(f32[128,256]{1,0:T(8,128)} %refs_4_.1) | copy-start | bytes 393220
  42.0 4.5 %collective-permute-start = (bf16[16,2,16,8,128]{4,3,2,1,0:T(8,128)(2,1)S(1)}, bf16[16,2,16,8,128]{4,3,2,1,0:T(8,128)(2,1)S(1)}, u32[]{:S(2)}, u32[]{:S(2)}) collective-permute-start(bf16[16,2,16,8,128]{4,3,2,1,0:T(8,128)(2,1)S(1)} %get-tuple-element.27.refs_0_), channel_id=1, source_target_pairs={{0,1},{1,0},{2,3},{3,2},{4,5},{5,4},{6,7},{7,6},{8,9},{9,8},{10,11... | collective-permute-start | bytes 3145736 | tf_op jit(solution)/shard_map/ppermute | solution.py:212

commit v7 on v6

--- a/solution.py
+++ b/solution.py
@@ -39,7 +39,8 @@
 
 
 def plane_visit(nx, ny, n_side):
-    pairs = [((nx // 2 - i) % nx, (ny // 2 - j) % ny) for j in range(ny) for i in range(nx)]
+    near = [((nx // 2 - i) % nx, (ny // 2 - j) % ny) for j in range(ny // 2) for i in range(nx)]
+    pairs = [pair for x, y in near for pair in ((x, y), ((x + nx // 2) % nx, (y + ny // 2) % ny))]
     return [(x * (ny // n_side) + y // n_side, y % n_side) for x, y in pairs]
 
 

time: 47.8 us -> 47.8 us (level)
  no operation moved by 1% of the time
where the time goes in v7:
time: 47.8 us; the launch traced here: 47.6 us
  blocking collectives  39.8 us (83%)
  Pallas kernels  4.2 us (9%)
  starting transfers between devices  1.91 us (4%)
  waiting for transfers between devices  0.86 us (2%)
  between operations  0.7 us (1%)
    all_to_all x1, blocking collectives, flipped_part(): lax.all_to_all(pieces, 'dp', 0, 0, tiled=True, axis_index_groups=groups)  16 us
    all_to_all x1, blocking collectives, flipped_part(): lax.all_to_all(copies, ('dp', 'tensor'), 0, 0, tiled=True, axis_index_gro...  15.2 us
    all_gather x1, blocking collectives, body(): lax.all_gather(own, 'tensor', axis=0, axis_index_groups=[[2 * k, 2 * k +...  8.51 us
    ppermute x1, starting transfers between devices, body(): other = lax.ppermute(mine, 'tensor', [(i, i ^ 1) for i in range(n_tensor)])  1.91 us
    pallas_call x1, Pallas kernels, body(): pl.pallas_call(lambda *refs: finish_kernel(orders, *refs), out_shape=(*ou...  1.72 us
    pallas_call x1, Pallas kernels, body(): pl.pallas_call(lambda *refs: flip_kernel(z_order, *refs), out_shape=pltpu...  1.35 us
  transfers between devices with their start and end apart: 1, of which 1 were waited for; matrix products, arithmetic and copies ran while one was open for 0% of the time, Pallas kernels for 4%

profile of v7, /device:TPU:1, one launch (start us, length us, event | category | flops | bytes accessed | tf_op | source)
XLA Modules:
  0.0 47.6 jit_solution(1140434120156611726)
XLA Ops:
  0.6 1.3 %flip.1 = bf16[512,128]{1,0:T(8,128)(2,1)S(1)} custom-call(f32[128,256]{1,0:T(8,128)} %refs_1_.3, f32[128,256]{1,0:T(8,128)} %refs_2_.3, f32[128,256]{1,0:T(8,128)} %refs_3_.3, f32[128,256]{1,0:T(8,128)} %refs_4_.1), custom_call_target="tpu_custom_call" | custom-call | flops 655360 | bytes 524288 | tf_op jit(solution)/shard_map/flip/pallas_call | solution.py:170
  2.0 8.5 %all-gather = bf16[1024,128]{1,0:T(8,128)(2,1)S(1)} all-gather(bf16[512,128]{1,0:T(8,128)(2,1)S(1)} %flip.1), channel_id=2, replica_groups={{0,1},{2,3},{4,5},{6,7},{8,9},{10,11},{12,13},{14,15},{16,17},{18,19},{..., dimensions={0}, use_global_device_ids=true | all-gather | bytes 393216 | tf_op jit(solution)/shard_map/all_gather | solution.py:179
  10.5 0.0 copy-start
  10.5 0.0 copy-start.1
  10.5 0.0 copy-start.2
  10.5 0.0 copy-start.3
  10.5 31.6 %conditional.1 = (bf16[16,2,16,8,128]{4,3,2,1,0:T(8,128)(2,1)S(1)}) conditional(s32[]{:T(128)} %convert_element_type.3, bf16[2,512,128]{2,1,0:T(8,128)(2,1)S(1)} %bitcast.20, bf16[2,512,128]{2,1,0:T(8,128)(2,1)S(1)} %bitcast.21), branch_computations={%region_0.1_spmd, %region_1.2_spmd} | conditional | bytes 3145736 | solution.py:212
  10.6 16.0 %all_to_all.13 = bf16[16,2,2,8,128]{4,3,2,1,0:T(8,128)(2,1)S(1)} all-to-all(bf16[16,2,2,8,128]{4,3,2,1,0:T(8,128)(2,1)S(1)} %copy.13), channel_id=1, replica_groups={{288,0,256,64,320,32,224,480,352,96,192,448,384,128,160,416},{304,16,27..., dimensions={0} | all-to-all | bytes 262144 | tf_op jit(solution)/shard_map/cond/branch_1_fun/all_to_all | solution.py:196
  26.6 0.2 spread.1
  26.8 15.2 %all_to_all.14 = bf16[16,2,16,8,128]{4,3,2,1,0:T(8,128)(2,1)S(1)} all-to-all(bf16[16,2,16,8,128]{4,3,2,1,0:T(8,128)(2,1)S(1)} %spread.1), channel_id=1, replica_groups={{10,0,6,12,2,8,14,4,24,18,20,30,16,26,28,22},{11,1,7,13,3,9,15,5,25,19,..., dimensions={0} | all-to-all | bytes 2097152 | tf_op jit(solution)/shard_map/cond/branch_1_fun/all_to_all | solution.py:207
  42.1 1.9 %collective-permute-start = (bf16[16,2,16,8,128]{4,3,2,1,0:T(8,128)(2,1)S(1)}, bf16[16,2,16,8,128]{4,3,2,1,0:T(8,128)(2,1)S(1)}, u32[]{:S(2)}, u32[]{:S(2)}) collective-permute-start(bf16[16,2,16,8,128]{4,3,2,1,0:T(8,128)(2,1)S(1)} %get-tuple-element.27.refs_0_), channel_id=1, source_target_pairs={{0,1},{1,0},{2,3},{3,2},{4,5},{5,4},{6,7},{7,6},{8,9},{9,8},{10,11... | collective-permute-start | bytes 3145736 | tf_op jit(solution)/shard_map/ppermute | solution.py:213
  44.0 0.0 copy-done
  44.0 0.0 copy-done.1
  44.0 0.0 copy-done.2
  44.0 0.0 copy-done.3
  44.0 1.7 %finish.1 = (bf16[16,8,4096]{2,1,0:T(8,128)(2,1)}, bf16[16,16,2,8,128]{4,3,2,1,0:T(8,128)(2,1)}, f32[128,256]{1,0:T(8,128)}, f32[128,256]{1,0:T(8,128)}, f32[128,256]{1,0:T(8,128)}, /*index=5*/f32[1,2]{1,0:T(1,128)}) custom-call(bf16[16,2,16,8,128]{4,3,2,1,0:T(8,128)(2,1)S(1)} %get-tuple-element.27.refs_0_, f32[128,256]{1,0:T(8,128)S(1)} %copy-done, ...), custom_call_target="tpu_custom_call" | custom-call | flops 655360 | bytes 2097152 | tf_op jit(solution)/shard_map/finish/pallas_call | solution.py:219
  45.8 0.9 %collective-permute-done.refs_0_ = bf16[16,2,16,8,128]{4,3,2,1,0:T(8,128)(2,1)S(1)} collective-permute-done((bf16[16,2,16,8,128]{4,3,2,1,0:T(8,128)(2,1)S(1)}, bf16[16,2,16,8,128]{4,3,2,1,0:T(8,128)(2,1)S(1)}, u32[]{:S(2)}, u32[]{:S(2)}) %collective-permute-start) | collective-permute-done | bytes 1048608 | tf_op jit(solution)/shard_map/ppermute | solution.py:213
  46.6 0.9 %place.1 = (bf16[16,8,4096]{2,1,0:T(8,128)(2,1)}, bf16[16,16,2,8,128]{4,3,2,1,0:T(8,128)(2,1)}) custom-call(bf16[16,2,16,8,128]{4,3,2,1,0:T(8,128)(2,1)S(1)} %collective-permute-done.refs_0_, bf16[16,8,4096]{2,1,0:T(8,128)(2,1)} %get-tuple-element.23.refs_1_, ...), custom_call_target="tpu_custom_call", output_to_operand_aliasing={{0}: (1, {}), {1}: (2, {})} | custom-call | bytes 2097152 | tf_op jit(solution)/shard_map/place/pallas_call | solution.py:228
  (3 shorter events, 0.1 us)
Async XLA Ops:
  10.5 33.5 %copy-start = (f32[128,256]{1,0:T(8,128)S(1)}, f32[128,256]{1,0:T(8,128)}, u32[]{:S(2)}) copy-start(f32[128,256]{1,0:T(8,128)} %refs_1_.3) | copy-start | bytes 393220
  10.5 33.5 %copy-start.1 = (f32[128,256]{1,0:T(8,128)S(1)}, f32[128,256]{1,0:T(8,128)}, u32[]{:S(2)}) copy-start(f32[128,256]{1,0:T(8,128)} %refs_2_.3) | copy-start | bytes 393220
  10.5 33.5 %copy-start.2 = (f32[128,256]{1,0:T(8,128)S(1)}, f32[128,256]{1,0:T(8,128)}, u32[]{:S(2)}) copy-start(f32[128,256]{1,0:T(8,128)} %refs_3_.3) | copy-start | bytes 393220
  10.5 33.5 %copy-start.3 = (f32[128,256]{1,0:T(8,128)S(1)}, f32[128,256]{1,0:T(8,128)}, u32[]{:S(2)}) copy-start(f32[128,256]{1,0:T(8,128)} %refs_4_.1) | copy-start | bytes 393220
  42.1 4.5 %collective-permute-start = (bf16[16,2,16,8,128]{4,3,2,1,0:T(8,128)(2,1)S(1)}, bf16[16,2,16,8,128]{4,3,2,1,0:T(8,128)(2,1)S(1)}, u32[]{:S(2)}, u32[]{:S(2)}) collective-permute-start(bf16[16,2,16,8,128]{4,3,2,1,0:T(8,128)(2,1)S(1)} %get-tuple-element.27.refs_0_), channel_id=1, source_target_pairs={{0,1},{1,0},{2,3},{3,2},{4,5},{5,4},{6,7},{7,6},{8,9},{9,8},{10,11... | collective-permute-start | bytes 3145736 | tf_op jit(solution)/shard_map/ppermute | solution.py:213
